TPU v7x, 32 devices: a whole 2x2x4 slice. The times are simulated.
32 devices in a mesh: tile: 8 (over z, x), func: 4 (over y, core).
Axes of the slice: x: 2, y: 2, z: 4, core: 2. Of those that a mesh axis runs over, the one named last changes fastest.
Arguments:
- seeds: float32 [12, 5, 256, 128], P('func', None, 'tile'), may hold values from -6 to 6
- checkpoints: float32 [2, 5, 256, 128], P(None, None, ('tile', 'func')), may hold values from -0.6 to 4.2, as said below
Outputs:
- adjoint_start: float32 [12, 5, 256, 128], P('func', None, 'tile')
Inputs may be any that keep to these rules, and one draw needn't show every extreme that they name: `checkpoints`: each checkpoint cell is a state with density between 1 and 1.5, each velocity component between -0.4 and 0.4, and pressure between 1 and 1.5.
All inputs are finite; a program needn't handle non-finite values.
Results may differ from a plain program's by a relative error of at most 0.00002.
Values sent between devices are 32-bit elements; how exact they have to be, the bound alone decides.
No kernel may reach another device: no remote copies, remote signals or barrier semaphores. Data moves between devices by JAX's collectives and lax.ppermute only.
A program may use at most 64 MiB of HBM per device.

v0:
```python
import jax
import jax.numpy as jnp
from jax import lax
from jax.sharding import PartitionSpec as P

NZ = 4
STEPS = 2


step_size = 0.3


def with_halo(cells, sides, width):
    for axis, dim in sides:
        count = lax.axis_size(axis)
        head = lax.slice_in_dim(cells, 0, width, axis=dim)
        tail = lax.slice_in_dim(cells, cells.shape[dim] - width, cells.shape[dim], axis=dim)
        cells = jnp.concatenate(
            [
                lax.ppermute(tail, axis, [(i, (i + 1) % count) for i in range(count)]),
                cells,
                lax.ppermute(head, axis, [((i + 1) % count, i) for i in range(count)]),
            ],
            axis=dim,
        )
    return cells


def trim_rows(field, depth):
    total = field.shape[-2]
    return lax.slice_in_dim(field, depth, total - depth, axis=field.ndim - 2)


def diff_trim(padded):
    inner_count = padded.shape[-2] - 4
    position = padded.ndim - 2

    def window_at(offset):
        return lax.slice_in_dim(padded, offset, offset + inner_count, axis=position)

    return (window_at(0) - window_at(4) + 8.0 * (window_at(3) - window_at(1))) / 12.0


def diff_second(field):
    return (
        jnp.roll(field, 2 * NZ, axis=-1)
        - jnp.roll(field, -2 * NZ, axis=-1)
        + 8.0 * (jnp.roll(field, -NZ, axis=-1) - jnp.roll(field, NZ, axis=-1))
    ) / 12.0


def pressure(state):
    density, mom_x, mom_y, mom_z, energy = (state[0], state[1], state[2], state[3], state[4])
    return 0.4 * (energy - (mom_x * mom_x + mom_y * mom_y + mom_z * mom_z) / (2.0 * density))


def flux_first(state):
    density, mom_x, mom_y, mom_z, energy = (state[0], state[1], state[2], state[3], state[4])
    speed = mom_x / density
    press = pressure(state)
    return jnp.stack(
        [mom_x, mom_x * speed + press, mom_y * speed, mom_z * speed, (energy + press) * speed]
    )


def flux_second(state):
    density, mom_x, mom_y, mom_z, energy = (state[0], state[1], state[2], state[3], state[4])
    speed = mom_y / density
    press = pressure(state)
    return jnp.stack(
        [mom_y, mom_x * speed, mom_y * speed + press, mom_z * speed, (energy + press) * speed]
    )


def rhs_trim(state):
    inner = trim_rows(state, 2)
    return -(diff_trim(flux_first(state)) + diff_second(flux_second(inner)))


def strip_sections(strip):
    padded = with_halo(strip, (("tile", 1),), 6)
    slope_one = rhs_trim(padded)
    section_two = trim_rows(padded, 2) + 0.5 * step_size * slope_one
    slope_two = rhs_trim(section_two)
    section_three = trim_rows(padded, 4) + 0.5 * step_size * slope_two
    slope_three = rhs_trim(section_three)
    section_four = trim_rows(padded, 6) + step_size * slope_three
    return (
        trim_rows(padded, 6),
        trim_rows(section_two, 4),
        trim_rows(section_three, 2),
        section_four,
    )


def section_pullback(state, cotangent):
    along_first = diff_trim(cotangent)
    along_second = diff_second(trim_rows(cotangent, 2))
    unused_one, pull_first = jax.vjp(flux_first, state)
    unused_two, pull_second = jax.vjp(flux_second, state)

    def apply_both(first_part, second_part):
        return pull_first(first_part)[0] + pull_second(second_part)[0]

    return jax.vmap(apply_both)(along_first, along_second)


def rimmed_pullback(state, cotangent):
    padded = with_halo(cotangent, (("tile", 2),), 2)
    return section_pullback(state, padded)


def local(seeds, checkpoints):
    adjoint = seeds
    for moment in reversed(range(STEPS)):
        strip = lax.all_gather(checkpoints[moment], "func", axis=1, tiled=True)
        section_one, section_two, section_three, section_four = strip_sections(strip)
        term_four = rimmed_pullback(section_four, step_size / 6.0 * adjoint)
        term_three = rimmed_pullback(
            section_three, step_size / 3.0 * adjoint + step_size * term_four
        )
        term_two = rimmed_pullback(
            section_two, step_size / 3.0 * adjoint + 0.5 * step_size * term_three
        )
        term_one = rimmed_pullback(
            section_one, step_size / 6.0 * adjoint + 0.5 * step_size * term_two
        )
        adjoint = adjoint + term_one + term_two + term_three + term_four
    return adjoint


def solution(mesh):
    return jax.shard_map(
        local,
        mesh=mesh,
        in_specs=(P("func", None, "tile", None), P(None, None, ("tile", "func"), None)),
        out_specs=P("func", None, "tile", None),
        check_vma=False,
    )
```

profile of v0, /device:TPU:0, one launch (start us, length us, event | category | flops | bytes accessed | tf_op | source)
XLA Modules:
  0.0 92.2 jit_solution(7488996970211944355)
XLA Ops:
  0.0 0.8 fusion.256
  0.8 6.2 %all-gather = f32[1,5,32,128]{3,2,1,0:T(8,128)S(1)} all-gather(f32[1,5,8,128]{3,2,1,0:T(8,128)S(1)} %get-tuple-element.512), channel_id=2, replica_groups=mesh['tile'=8,'func'=4] {'func'}, dimensions={2}, use_global_device_ids=true | all-gather | bytes 102400 | tf_op jit(solution)/shard_map/all_gather | solution.py:116
  7.0 5.0 %collective-permute-start.3 = (f32[5,6,128]{2,1,0:T(8,128)S(1)}, f32[5,6,128]{2,1,0:T(8,128)S(1)}, u32[]{:S(2)}, u32[]{:S(2)}) collective-permute-start(f32[5,6,128]{2,1,0:T(8,128)S(1)} %get-tuple-element.446), channel_id=1, source_target_pairs={{4,0},{8,4},{12,8},{16,12},{20,16},{24,20},{28,24},{0,28},{5,1},{9... | collective-permute-start | bytes 46088 | tf_op jit(solution)/shard_map/ppermute | solution.py:22
  12.1 4.8 %collective-permute-start.1 = (f32[3,5,2,128]{3,2,1,0:T(2,128)S(1)}, f32[3,5,2,128]{3,2,1,0:T(2,128)S(1)}, u32[]{:S(2)}, u32[]{:S(2)}) collective-permute-start(f32[3,5,2,128]{3,2,1,0:T(2,128)S(1)} %get-tuple-element.276), channel_id=1, source_target_pairs={{4,0},{8,4},{12,8},{16,12},{20,16},{24,20},{28,24},{0,28},{5,1},{9... | collective-permute-start | bytes 46088 | tf_op jit(solution)/shard_map/ppermute | solution.py:22
  16.9 5.3 %all-gather.1 = f32[1,5,32,128]{3,2,1,0:T(8,128)S(1)} all-gather(f32[1,5,8,128]{3,2,1,0:T(8,128)S(1)} %get-tuple-element.511), channel_id=3, replica_groups=mesh['tile'=8,'func'=4] {'func'}, dimensions={2}, use_global_device_ids=true | all-gather | bytes 102400 | tf_op jit(solution)/shard_map/all_gather | solution.py:116
  22.2 4.7 %collective-permute-start.13 = (f32[5,6,128]{2,1,0:T(8,128)S(1)}, f32[5,6,128]{2,1,0:T(8,128)S(1)}, u32[]{:S(2)}, u32[]{:S(2)}) collective-permute-start(f32[5,6,128]{2,1,0:T(8,128)S(1)} %get-tuple-element.409), channel_id=1, source_target_pairs={{4,0},{8,4},{12,8},{16,12},{20,16},{24,20},{28,24},{0,28},{5,1},{9... | collective-permute-start | bytes 46088 | tf_op jit(solution)/shard_map/ppermute | solution.py:22
  27.6 0.3 fusion.57
  28.6 0.2 fusion.107
  29.4 0.2 fusion.100
  30.1 0.2 fusion.129
  30.7 0.1 multiply_add_fusion.5
  31.5 3.0 %collective-permute-done.12 = f32[5,6,128]{2,1,0:T(8,128)S(1)} collective-permute-done((f32[5,6,128]{2,1,0:T(8,128)S(1)}, f32[5,6,128]{2,1,0:T(8,128)S(1)}, u32[]{:S(2)}, u32[]{:S(2)}) %collective-permute-start.12) | collective-permute-done | bytes 15392 | tf_op jit(solution)/shard_map/ppermute | solution.py:20
  35.1 0.2 fusion.93
  35.8 0.2 fusion.86
  36.6 0.2 fusion.122
  36.9 1.8 %collective-permute-start.5 = (f32[3,5,2,128]{3,2,1,0:T(2,128)S(1)}, f32[3,5,2,128]{3,2,1,0:T(2,128)S(1)}, u32[]{:S(2)}, u32[]{:S(2)}) collective-permute-start(f32[3,5,2,128]{3,2,1,0:T(2,128)S(1)} %get-tuple-element.266), channel_id=1, source_target_pairs={{4,0},{8,4},{12,8},{16,12},{20,16},{24,20},{28,24},{0,28},{5,1},{9... | collective-permute-start | bytes 46088 | tf_op jit(solution)/shard_map/ppermute | solution.py:22
  38.6 0.3 collective-permute-start.4
  38.9 0.3 fusion.60
  39.3 1.4 %collective-permute-done.5 = f32[3,5,2,128]{3,2,1,0:T(2,128)S(1)} collective-permute-done((f32[3,5,2,128]{3,2,1,0:T(2,128)S(1)}, f32[3,5,2,128]{3,2,1,0:T(2,128)S(1)}, u32[]{:S(2)}, u32[]{:S(2)}) %collective-permute-start.5) | collective-permute-done | bytes 15392 | tf_op jit(solution)/shard_map/ppermute | solution.py:22
  40.6 4.4 %collective-permute-done.4 = f32[3,5,2,128]{3,2,1,0:T(2,128)S(1)} collective-permute-done((f32[3,5,2,128]{3,2,1,0:T(2,128)S(1)}, f32[3,5,2,128]{3,2,1,0:T(2,128)S(1)}, u32[]{:S(2)}, u32[]{:S(2)}) %collective-permute-start.4) | collective-permute-done | bytes 15392 | tf_op jit(solution)/shard_map/ppermute | solution.py:20
  45.4 0.1 multiply_add_fusion.4
  46.2 2.0 %collective-permute-start.6 = (f32[3,5,2,128]{3,2,1,0:T(2,128)S(1)}, f32[3,5,2,128]{3,2,1,0:T(2,128)S(1)}, u32[]{:S(2)}, u32[]{:S(2)}) collective-permute-start(f32[3,5,2,128]{3,2,1,0:T(2,128)S(1)} %get-tuple-element.255), channel_id=1, source_target_pairs={{0,4},{4,8},{8,12},{12,16},{16,20},{20,24},{24,28},{28,0},{1,5},{5... | collective-permute-start | bytes 46088 | tf_op jit(solution)/shard_map/ppermute | solution.py:20
  48.2 0.3 fusion.63
  48.5 1.4 %collective-permute-done.7 = f32[3,5,2,128]{3,2,1,0:T(2,128)S(1)} collective-permute-done((f32[3,5,2,128]{3,2,1,0:T(2,128)S(1)}, f32[3,5,2,128]{3,2,1,0:T(2,128)S(1)}, u32[]{:S(2)}, u32[]{:S(2)}) %collective-permute-start.7) | collective-permute-done | bytes 15392 | tf_op jit(solution)/shard_map/ppermute | solution.py:22
  49.9 2.8 %collective-permute-done.6 = f32[3,5,2,128]{3,2,1,0:T(2,128)S(1)} collective-permute-done((f32[3,5,2,128]{3,2,1,0:T(2,128)S(1)}, f32[3,5,2,128]{3,2,1,0:T(2,128)S(1)}, u32[]{:S(2)}, u32[]{:S(2)}) %collective-permute-start.6) | collective-permute-done | bytes 15392 | tf_op jit(solution)/shard_map/ppermute | solution.py:20
  53.0 0.1 multiply_add_fusion.3
  53.8 2.0 %collective-permute-start.8 = (f32[3,5,2,128]{3,2,1,0:T(2,128)S(1)}, f32[3,5,2,128]{3,2,1,0:T(2,128)S(1)}, u32[]{:S(2)}, u32[]{:S(2)}) collective-permute-start(f32[3,5,2,128]{3,2,1,0:T(2,128)S(1)} %get-tuple-element.245), channel_id=1, source_target_pairs={{0,4},{4,8},{8,12},{12,16},{16,20},{20,24},{24,28},{28,0},{1,5},{5... | collective-permute-start | bytes 46088 | tf_op jit(solution)/shard_map/ppermute | solution.py:20
  55.8 0.3 fusion.66
  56.1 1.4 %collective-permute-done.9 = f32[3,5,2,128]{3,2,1,0:T(2,128)S(1)} collective-permute-done((f32[3,5,2,128]{3,2,1,0:T(2,128)S(1)}, f32[3,5,2,128]{3,2,1,0:T(2,128)S(1)}, u32[]{:S(2)}, u32[]{:S(2)}) %collective-permute-start.9) | collective-permute-done | bytes 15392 | tf_op jit(solution)/shard_map/ppermute | solution.py:22
  57.5 2.9 %collective-permute-done.8 = f32[3,5,2,128]{3,2,1,0:T(2,128)S(1)} collective-permute-done((f32[3,5,2,128]{3,2,1,0:T(2,128)S(1)}, f32[3,5,2,128]{3,2,1,0:T(2,128)S(1)}, u32[]{:S(2)}, u32[]{:S(2)}) %collective-permute-start.8) | collective-permute-done | bytes 15392 | tf_op jit(solution)/shard_map/ppermute | solution.py:20
  60.7 0.2 broadcast_multiply_fusion
  61.5 2.0 %collective-permute-start.10 = (f32[3,5,2,128]{3,2,1,0:T(2,128)S(1)}, f32[3,5,2,128]{3,2,1,0:T(2,128)S(1)}, u32[]{:S(2)}, u32[]{:S(2)}) collective-permute-start(f32[3,5,2,128]{3,2,1,0:T(2,128)S(1)} %get-tuple-element.235), channel_id=1, source_target_pairs={{0,4},{4,8},{8,12},{12,16},{16,20},{20,24},{24,28},{28,0},{1,5},{5... | collective-permute-start | bytes 46088 | tf_op jit(solution)/shard_map/ppermute | solution.py:20
  63.5 0.3 fusion.69
  63.9 1.4 %collective-permute-done.11 = f32[3,5,2,128]{3,2,1,0:T(2,128)S(1)} collective-permute-done((f32[3,5,2,128]{3,2,1,0:T(2,128)S(1)}, f32[3,5,2,128]{3,2,1,0:T(2,128)S(1)}, u32[]{:S(2)}, u32[]{:S(2)}) %collective-permute-start.11) | collective-permute-done | bytes 15392 | tf_op jit(solution)/shard_map/ppermute | solution.py:22
  65.2 2.8 %collective-permute-done.10 = f32[3,5,2,128]{3,2,1,0:T(2,128)S(1)} collective-permute-done((f32[3,5,2,128]{3,2,1,0:T(2,128)S(1)}, f32[3,5,2,128]{3,2,1,0:T(2,128)S(1)}, u32[]{:S(2)}, u32[]{:S(2)}) %collective-permute-start.10) | collective-permute-done | bytes 15392 | tf_op jit(solution)/shard_map/ppermute | solution.py:20
  69.1 2.0 %collective-permute-start.14 = (f32[3,5,2,128]{3,2,1,0:T(2,128)S(1)}, f32[3,5,2,128]{3,2,1,0:T(2,128)S(1)}, u32[]{:S(2)}, u32[]{:S(2)}) collective-permute-start(f32[3,5,2,128]{3,2,1,0:T(2,128)S(1)} %get-tuple-element.225), channel_id=1, source_target_pairs={{0,4},{4,8},{8,12},{12,16},{16,20},{20,24},{24,28},{28,0},{1,5},{5... | collective-permute-start | bytes 46088 | tf_op jit(solution)/shard_map/ppermute | solution.py:20
  71.1 0.3 fusion.72
  71.5 1.4 %collective-permute-done.15 = f32[3,5,2,128]{3,2,1,0:T(2,128)S(1)} collective-permute-done((f32[3,5,2,128]{3,2,1,0:T(2,128)S(1)}, f32[3,5,2,128]{3,2,1,0:T(2,128)S(1)}, u32[]{:S(2)}, u32[]{:S(2)}) %collective-permute-start.15) | collective-permute-done | bytes 15392 | tf_op jit(solution)/shard_map/ppermute | solution.py:22
  72.8 2.9 %collective-permute-done.14 = f32[3,5,2,128]{3,2,1,0:T(2,128)S(1)} collective-permute-done((f32[3,5,2,128]{3,2,1,0:T(2,128)S(1)}, f32[3,5,2,128]{3,2,1,0:T(2,128)S(1)}, u32[]{:S(2)}, u32[]{:S(2)}) %collective-permute-start.14) | collective-permute-done | bytes 15392 | tf_op jit(solution)/shard_map/ppermute | solution.py:20
  76.9 2.0 %collective-permute-start.16 = (f32[3,5,2,128]{3,2,1,0:T(2,128)S(1)}, f32[3,5,2,128]{3,2,1,0:T(2,128)S(1)}, u32[]{:S(2)}, u32[]{:S(2)}) collective-permute-start(f32[3,5,2,128]{3,2,1,0:T(2,128)S(1)} %get-tuple-element.215), channel_id=1, source_target_pairs={{0,4},{4,8},{8,12},{12,16},{16,20},{20,24},{24,28},{28,0},{1,5},{5... | collective-permute-start | bytes 46088 | tf_op jit(solution)/shard_map/ppermute | solution.py:20
  78.9 0.3 fusion.75
  79.2 1.4 %collective-permute-done.17 = f32[3,5,2,128]{3,2,1,0:T(2,128)S(1)} collective-permute-done((f32[3,5,2,128]{3,2,1,0:T(2,128)S(1)}, f32[3,5,2,128]{3,2,1,0:T(2,128)S(1)}, u32[]{:S(2)}, u32[]{:S(2)}) %collective-permute-start.17) | collective-permute-done | bytes 15392 | tf_op jit(solution)/shard_map/ppermute | solution.py:22
  80.6 2.8 %collective-permute-done.16 = f32[3,5,2,128]{3,2,1,0:T(2,128)S(1)} collective-permute-done((f32[3,5,2,128]{3,2,1,0:T(2,128)S(1)}, f32[3,5,2,128]{3,2,1,0:T(2,128)S(1)}, u32[]{:S(2)}, u32[]{:S(2)}) %collective-permute-start.16) | collective-permute-done | bytes 15392 | tf_op jit(solution)/shard_map/ppermute | solution.py:20
  84.5 2.0 %collective-permute-start.18 = (f32[3,5,2,128]{3,2,1,0:T(2,128)S(1)}, f32[3,5,2,128]{3,2,1,0:T(2,128)S(1)}, u32[]{:S(2)}, u32[]{:S(2)}) collective-permute-start(f32[3,5,2,128]{3,2,1,0:T(2,128)S(1)} %get-tuple-element.205), channel_id=1, source_target_pairs={{0,4},{4,8},{8,12},{12,16},{16,20},{20,24},{24,28},{28,0},{1,5},{5... | collective-permute-start | bytes 46088 | tf_op jit(solution)/shard_map/ppermute | solution.py:20
  86.5 0.3 fusion.78
  86.8 1.4 %collective-permute-done.19 = f32[3,5,2,128]{3,2,1,0:T(2,128)S(1)} collective-permute-done((f32[3,5,2,128]{3,2,1,0:T(2,128)S(1)}, f32[3,5,2,128]{3,2,1,0:T(2,128)S(1)}, u32[]{:S(2)}, u32[]{:S(2)}) %collective-permute-start.19) | collective-permute-done | bytes 15392 | tf_op jit(solution)/shard_map/ppermute | solution.py:22
  88.2 2.8 %collective-permute-done.18 = f32[3,5,2,128]{3,2,1,0:T(2,128)S(1)} collective-permute-done((f32[3,5,2,128]{3,2,1,0:T(2,128)S(1)}, f32[3,5,2,128]{3,2,1,0:T(2,128)S(1)}, u32[]{:S(2)}, u32[]{:S(2)}) %collective-permute-start.18) | collective-permute-done | bytes 15392 | tf_op jit(solution)/shard_map/ppermute | solution.py:20
  91.3 0.9 add_add_fusion
  (203 shorter events, 10.5 us)
Async XLA Ops:
  0.0 12.1 %copy-start = (f32[3,5,32,128]{3,2,1,0:T(8,128)S(1)}, f32[3,5,32,128]{3,2,1,0:T(8,128)}, u32[]{:S(2)}) copy-start(f32[3,5,32,128]{3,2,1,0:T(8,128)} %param.2) | copy-start | bytes 737284
  7.0 20.9 %collective-permute-start.3 = (f32[5,6,128]{2,1,0:T(8,128)S(1)}, f32[5,6,128]{2,1,0:T(8,128)S(1)}, u32[]{:S(2)}, u32[]{:S(2)}) collective-permute-start(f32[5,6,128]{2,1,0:T(8,128)S(1)} %get-tuple-element.446), channel_id=1, source_target_pairs={{4,0},{8,4},{12,8},{16,12},{20,16},{24,20},{28,24},{0,28},{5,1},{9... | collective-permute-start | bytes 46088 | tf_op jit(solution)/shard_map/ppermute | solution.py:22
  12.1 15.9 %collective-permute-start.2 = (f32[5,6,128]{2,1,0:T(8,128)S(1)}, f32[5,6,128]{2,1,0:T(8,128)S(1)}, u32[]{:S(2)}, u32[]{:S(2)}) collective-permute-start(f32[5,6,128]{2,1,0:T(8,128)S(1)} %get-tuple-element.445), channel_id=1, source_target_pairs={{0,4},{4,8},{8,12},{12,16},{16,20},{20,24},{24,28},{28,0},{1,5},{5... | collective-permute-start | bytes 46088 | tf_op jit(solution)/shard_map/ppermute | solution.py:20
  12.1 18.2 %collective-permute-start.1 = (f32[3,5,2,128]{3,2,1,0:T(2,128)S(1)}, f32[3,5,2,128]{3,2,1,0:T(2,128)S(1)}, u32[]{:S(2)}, u32[]{:S(2)}) collective-permute-start(f32[3,5,2,128]{3,2,1,0:T(2,128)S(1)} %get-tuple-element.276), channel_id=1, source_target_pairs={{4,0},{8,4},{12,8},{16,12},{20,16},{24,20},{28,24},{0,28},{5,1},{9... | collective-permute-start | bytes 46088 | tf_op jit(solution)/shard_map/ppermute | solution.py:22
  16.9 13.5 %collective-permute-start = (f32[3,5,2,128]{3,2,1,0:T(2,128)S(1)}, f32[3,5,2,128]{3,2,1,0:T(2,128)S(1)}, u32[]{:S(2)}, u32[]{:S(2)}) collective-permute-start(f32[3,5,2,128]{3,2,1,0:T(2,128)S(1)} %get-tuple-element.275), channel_id=1, source_target_pairs={{0,4},{4,8},{8,12},{12,16},{16,20},{20,24},{24,28},{28,0},{1,5},{5... | collective-permute-start | bytes 46088 | tf_op jit(solution)/shard_map/ppermute | solution.py:20
  22.2 9.3 %collective-permute-start.13 = (f32[5,6,128]{2,1,0:T(8,128)S(1)}, f32[5,6,128]{2,1,0:T(8,128)S(1)}, u32[]{:S(2)}, u32[]{:S(2)}) collective-permute-start(f32[5,6,128]{2,1,0:T(8,128)S(1)} %get-tuple-element.409), channel_id=1, source_target_pairs={{4,0},{8,4},{12,8},{16,12},{20,16},{24,20},{28,24},{0,28},{5,1},{9... | collective-permute-start | bytes 46088 | tf_op jit(solution)/shard_map/ppermute | solution.py:22
  27.9 6.5 %collective-permute-start.12 = (f32[5,6,128]{2,1,0:T(8,128)S(1)}, f32[5,6,128]{2,1,0:T(8,128)S(1)}, u32[]{:S(2)}, u32[]{:S(2)}) collective-permute-start(f32[5,6,128]{2,1,0:T(8,128)S(1)} %get-tuple-element.408), channel_id=1, source_target_pairs={{0,4},{4,8},{8,12},{12,16},{16,20},{20,24},{24,28},{28,0},{1,5},{5... | collective-permute-start | bytes 46088 | tf_op jit(solution)/shard_map/ppermute | solution.py:20
  36.9 3.8 %collective-permute-start.5 = (f32[3,5,2,128]{3,2,1,0:T(2,128)S(1)}, f32[3,5,2,128]{3,2,1,0:T(2,128)S(1)}, u32[]{:S(2)}, u32[]{:S(2)}) collective-permute-start(f32[3,5,2,128]{3,2,1,0:T(2,128)S(1)} %get-tuple-element.266), channel_id=1, source_target_pairs={{4,0},{8,4},{12,8},{16,12},{20,16},{24,20},{28,24},{0,28},{5,1},{9... | collective-permute-start | bytes 46088 | tf_op jit(solution)/shard_map/ppermute | solution.py:22
  38.6 6.4 %collective-permute-start.4 = (f32[3,5,2,128]{3,2,1,0:T(2,128)S(1)}, f32[3,5,2,128]{3,2,1,0:T(2,128)S(1)}, u32[]{:S(2)}, u32[]{:S(2)}) collective-permute-start(f32[3,5,2,128]{3,2,1,0:T(2,128)S(1)} %get-tuple-element.265), channel_id=1, source_target_pairs={{0,4},{4,8},{8,12},{12,16},{16,20},{20,24},{24,28},{28,0},{1,5},{5... | collective-permute-start | bytes 46088 | tf_op jit(solution)/shard_map/ppermute | solution.py:20
  46.1 3.8 %collective-permute-start.7 = (f32[3,5,2,128]{3,2,1,0:T(2,128)S(1)}, f32[3,5,2,128]{3,2,1,0:T(2,128)S(1)}, u32[]{:S(2)}, u32[]{:S(2)}) collective-permute-start(f32[3,5,2,128]{3,2,1,0:T(2,128)S(1)} %get-tuple-element.256), channel_id=1, source_target_pairs={{4,0},{8,4},{12,8},{16,12},{20,16},{24,20},{28,24},{0,28},{5,1},{9... | collective-permute-start | bytes 46088 | tf_op jit(solution)/shard_map/ppermute | solution.py:22
  46.2 6.5 %collective-permute-start.6 = (f32[3,5,2,128]{3,2,1,0:T(2,128)S(1)}, f32[3,5,2,128]{3,2,1,0:T(2,128)S(1)}, u32[]{:S(2)}, u32[]{:S(2)}) collective-permute-start(f32[3,5,2,128]{3,2,1,0:T(2,128)S(1)} %get-tuple-element.255), channel_id=1, source_target_pairs={{0,4},{4,8},{8,12},{12,16},{16,20},{20,24},{24,28},{28,0},{1,5},{5... | collective-permute-start | bytes 46088 | tf_op jit(solution)/shard_map/ppermute | solution.py:20
  53.7 3.8 %collective-permute-start.9 = (f32[3,5,2,128]{3,2,1,0:T(2,128)S(1)}, f32[3,5,2,128]{3,2,1,0:T(2,128)S(1)}, u32[]{:S(2)}, u32[]{:S(2)}) collective-permute-start(f32[3,5,2,128]{3,2,1,0:T(2,128)S(1)} %get-tuple-element.246), channel_id=1, source_target_pairs={{4,0},{8,4},{12,8},{16,12},{20,16},{24,20},{28,24},{0,28},{5,1},{9... | collective-permute-start | bytes 46088 | tf_op jit(solution)/shard_map/ppermute | solution.py:22
  53.8 6.6 %collective-permute-start.8 = (f32[3,5,2,128]{3,2,1,0:T(2,128)S(1)}, f32[3,5,2,128]{3,2,1,0:T(2,128)S(1)}, u32[]{:S(2)}, u32[]{:S(2)}) collective-permute-start(f32[3,5,2,128]{3,2,1,0:T(2,128)S(1)} %get-tuple-element.245), channel_id=1, source_target_pairs={{0,4},{4,8},{8,12},{12,16},{16,20},{20,24},{24,28},{28,0},{1,5},{5... | collective-permute-start | bytes 46088 | tf_op jit(solution)/shard_map/ppermute | solution.py:20
  61.5 3.8 %collective-permute-start.11 = (f32[3,5,2,128]{3,2,1,0:T(2,128)S(1)}, f32[3,5,2,128]{3,2,1,0:T(2,128)S(1)}, u32[]{:S(2)}, u32[]{:S(2)}) collective-permute-start(f32[3,5,2,128]{3,2,1,0:T(2,128)S(1)} %get-tuple-element.236), channel_id=1, source_target_pairs={{4,0},{8,4},{12,8},{16,12},{20,16},{24,20},{28,24},{0,28},{5,1},{9... | collective-permute-start | bytes 46088 | tf_op jit(solution)/shard_map/ppermute | solution.py:22
  61.5 6.5 %collective-permute-start.10 = (f32[3,5,2,128]{3,2,1,0:T(2,128)S(1)}, f32[3,5,2,128]{3,2,1,0:T(2,128)S(1)}, u32[]{:S(2)}, u32[]{:S(2)}) collective-permute-start(f32[3,5,2,128]{3,2,1,0:T(2,128)S(1)} %get-tuple-element.235), channel_id=1, source_target_pairs={{0,4},{4,8},{8,12},{12,16},{16,20},{20,24},{24,28},{28,0},{1,5},{5... | collective-permute-start | bytes 46088 | tf_op jit(solution)/shard_map/ppermute | solution.py:20
  69.0 3.8 %collective-permute-start.15 = (f32[3,5,2,128]{3,2,1,0:T(2,128)S(1)}, f32[3,5,2,128]{3,2,1,0:T(2,128)S(1)}, u32[]{:S(2)}, u32[]{:S(2)}) collective-permute-start(f32[3,5,2,128]{3,2,1,0:T(2,128)S(1)} %get-tuple-element.226), channel_id=1, source_target_pairs={{4,0},{8,4},{12,8},{16,12},{20,16},{24,20},{28,24},{0,28},{5,1},{9... | collective-permute-start | bytes 46088 | tf_op jit(solution)/shard_map/ppermute | solution.py:22
  69.1 6.7 %collective-permute-start.14 = (f32[3,5,2,128]{3,2,1,0:T(2,128)S(1)}, f32[3,5,2,128]{3,2,1,0:T(2,128)S(1)}, u32[]{:S(2)}, u32[]{:S(2)}) collective-permute-start(f32[3,5,2,128]{3,2,1,0:T(2,128)S(1)} %get-tuple-element.225), channel_id=1, source_target_pairs={{0,4},{4,8},{8,12},{12,16},{16,20},{20,24},{24,28},{28,0},{1,5},{5... | collective-permute-start | bytes 46088 | tf_op jit(solution)/shard_map/ppermute | solution.py:20
  76.8 3.8 %collective-permute-start.17 = (f32[3,5,2,128]{3,2,1,0:T(2,128)S(1)}, f32[3,5,2,128]{3,2,1,0:T(2,128)S(1)}, u32[]{:S(2)}, u32[]{:S(2)}) collective-permute-start(f32[3,5,2,128]{3,2,1,0:T(2,128)S(1)} %get-tuple-element.216), channel_id=1, source_target_pairs={{4,0},{8,4},{12,8},{16,12},{20,16},{24,20},{28,24},{0,28},{5,1},{9... | collective-permute-start | bytes 46088 | tf_op jit(solution)/shard_map/ppermute | solution.py:22
  76.9 6.5 %collective-permute-start.16 = (f32[3,5,2,128]{3,2,1,0:T(2,128)S(1)}, f32[3,5,2,128]{3,2,1,0:T(2,128)S(1)}, u32[]{:S(2)}, u32[]{:S(2)}) collective-permute-start(f32[3,5,2,128]{3,2,1,0:T(2,128)S(1)} %get-tuple-element.215), channel_id=1, source_target_pairs={{0,4},{4,8},{8,12},{12,16},{16,20},{20,24},{24,28},{28,0},{1,5},{5... | collective-permute-start | bytes 46088 | tf_op jit(solution)/shard_map/ppermute | solution.py:20
  84.4 3.8 %collective-permute-start.19 = (f32[3,5,2,128]{3,2,1,0:T(2,128)S(1)}, f32[3,5,2,128]{3,2,1,0:T(2,128)S(1)}, u32[]{:S(2)}, u32[]{:S(2)}) collective-permute-start(f32[3,5,2,128]{3,2,1,0:T(2,128)S(1)} %get-tuple-element.206), channel_id=1, source_target_pairs={{4,0},{8,4},{12,8},{16,12},{20,16},{24,20},{28,24},{0,28},{5,1},{9... | collective-permute-start | bytes 46088 | tf_op jit(solution)/shard_map/ppermute | solution.py:22
  84.5 6.5 %collective-permute-start.18 = (f32[3,5,2,128]{3,2,1,0:T(2,128)S(1)}, f32[3,5,2,128]{3,2,1,0:T(2,128)S(1)}, u32[]{:S(2)}, u32[]{:S(2)}) collective-permute-start(f32[3,5,2,128]{3,2,1,0:T(2,128)S(1)} %get-tuple-element.205), channel_id=1, source_target_pairs={{0,4},{4,8},{8,12},{12,16},{16,20},{20,24},{24,28},{28,0},{1,5},{5... | collective-permute-start | bytes 46088 | tf_op jit(solution)/shard_map/ppermute | solution.py:20
where the time goes:
time: 92.3 us; the launch traced here: 92.2 us
  waiting for transfers between devices  33.9 us (37%)
  starting transfers between devices  29.1 us (32%)
  blocking collectives  11.5 us (12%)
  other arithmetic  8.91 us (10%)
  local copies, waits for them, and re-layouts  7.21 us (8%)
  between operations  1.52 us (2%)
    ppermute x10, waiting for transfers between devices, with_halo(): lax.ppermute(tail, axis, [(i, (i + 1) % count) for i in range(count)])  24.3 us
    ppermute x10, starting transfers between devices, with_halo(): lax.ppermute(head, axis, [((i + 1) % count, i) for i in range(count)])  16.7 us
    ppermute x10, starting transfers between devices, with_halo(): lax.ppermute(tail, axis, [(i, (i + 1) % count) for i in range(count)])  12.5 us
    all_gather x2, blocking collectives, local(): strip = lax.all_gather(checkpoints[moment], 'func', axis=1, tiled=True)  11.5 us
    ppermute x10, waiting for transfers between devices, with_halo(): lax.ppermute(head, axis, [((i + 1) % count, i) for i in range(count)])  9.63 us
    slice x28, local copies, waits for them, and re-layouts, diff_second(): jnp.roll(field, NZ, axis=-1)  3.15 us
    slice x28, local copies, waits for them, and re-layouts, diff_second(): jnp.roll(field, -2 * NZ, axis=-1)  3.09 us
    div x8, other arithmetic, diff_second(): (jnp.roll(field, 2 * NZ, axis=-1) - jnp.roll(field, -2 * NZ, axis=-1) + 8...  2.59 us
  transfers between devices with their start and end apart: 20, of which 15 were waited for; matrix products, arithmetic and copies ran while one was open for 7% of the time, Pallas kernels for 0%

commit v1 on v0

v1 whole, which is shorter than its diff:
```python
import jax
import jax.numpy as jnp
from jax import lax
from jax.experimental import pallas as pl
from jax.experimental.pallas import tpu as pltpu
from jax.sharding import PartitionSpec as P

NZ = 4
STEPS = 2
FIELDS = 5
LANES = 128
SUB = 8

step_size = 0.3
twelfth = step_size / 12.0

RIM = 16
BASE_RIM = 24


def swap_near(cells):
    count = lax.axis_size("tile")
    return lax.ppermute(cells, "tile", [(i, i ^ 1) for i in range(count)])


def swap_far(cells):
    count = lax.axis_size("tile")
    pairs = [(i, (i + (1 if i % 2 else -1)) % count) for i in range(count)]
    return lax.ppermute(cells, "tile", pairs)


def turn(cells, places, axis):
    return pltpu.roll(cells, places % cells.shape[axis], axis)


def diff_second(field):
    wide = turn(field, -2 * NZ, 1) - field
    return 8.0 * turn(wide, NZ, 1) - (wide + turn(wide, 2 * NZ, 1))


def diff_first(back_two, back_one, next_one, next_two):
    return 8.0 * (next_one - back_one) - (next_two - back_two)


class Column:
    def __init__(self, load, depth):
        self.load, self.depth, self.held = load, depth, {}

    def __getitem__(self, place):
        if place not in self.held:
            if place < 0:
                cells = turn(self[place + self.depth], 1, 0)
            elif place >= self.depth:
                cells = turn(self[place - self.depth], -1, 0)
            else:
                cells = self.load(place)
            self.held[place] = cells
        return self.held[place]

    def diff(self, place):
        return diff_first(self[place - 2], self[place - 1], self[place + 1], self[place + 2])


def primitives(state):
    density, mom_x, mom_y, mom_z, energy = state
    inverse = 1.0 / density
    vel_x, vel_y, vel_z = mom_x * inverse, mom_y * inverse, mom_z * inverse
    half = 0.5 * (vel_x * vel_x + vel_y * vel_y + vel_z * vel_z)
    press = 0.4 * (energy - density * half)
    total = energy + press
    return vel_x, vel_y, vel_z, total * inverse, half, press, total


def state_stages(moment, base_ref, coef_ref, now_ref, flux_ref, slope_ref, depth):
    def rows(place):
        return pl.ds(place, SUB, stride=depth)

    for stage in range(4):
        for j in range(depth):
            if stage == 0:
                state = [base_ref[moment, k, rows(j), :] for k in range(FIELDS)]
            else:
                state = [now_ref[k, j] for k in range(FIELDS)]
            vel_x, vel_y, vel_z, heat, half, press, total = primitives(state)
            for k, cells in enumerate((vel_x, vel_y, vel_z, heat, half)):
                coef_ref[stage, k, rows(j), :] = cells
            if stage == 3:
                continue
            _, mom_x, mom_y, mom_z, _ = state
            cross = mom_x * vel_y
            first = (mom_x, mom_x * vel_x + press, cross, mom_z * vel_x, total * vel_x)
            second = (mom_y, cross, mom_y * vel_y + press, mom_z * vel_y, total * vel_y)
            for k in range(FIELDS):
                flux_ref[k, j] = first[k]
                slope_ref[k, j] = diff_second(second[k])
        if stage == 3:
            return
        scale = (0.5 if stage < 2 else 1.0) * twelfth
        for k in range(FIELDS):
            column = Column(lambda place, k=k: flux_ref[k, place], depth)
            for j in range(depth):
                slope = column.diff(j) + slope_ref[k, j]
                now_ref[k, j] = base_ref[moment, k, rows(j), :] - scale * slope


def pull_stages(one, coef_ref, adj_ref, acc_ref, hold_ref, depth):
    shift = BASE_RIM - RIM
    for stage in (3, 2, 1, 0):
        source = (adj_ref.at[one], hold_ref.at[0], hold_ref.at[1], hold_ref.at[0])[3 - stage]
        columns = [Column(lambda place, k=k: source[k, place], depth) for k in range(FIELDS)]
        for j in range(depth):
            vel_x, vel_y, vel_z, heat, half = [
                coef_ref[stage, k, pl.ds(shift + j, SUB, stride=depth), :] for k in range(5)
            ]
            a = [column.diff(j) for column in columns]
            b = [diff_second(column[j]) for column in columns]
            mix_x = vel_x * a[1] + vel_y * a[2] + vel_z * a[3] + heat * a[4]
            mix_y = vel_x * b[1] + vel_y * b[2] + vel_z * b[3] + heat * b[4]
            lift = vel_x * a[4] + vel_y * b[4]
            press = 0.4 * (a[1] + b[2] + lift)
            term = (
                half * press - vel_x * mix_x - vel_y * mix_y,
                a[0] + mix_x + vel_x * (a[1] - press) + vel_y * b[1],
                b[0] + mix_y + vel_y * (b[2] - press) + vel_x * a[2],
                vel_x * a[3] + vel_y * b[3] - vel_z * press,
                lift + press,
            )
            for k in range(FIELDS):
                if stage == 3:
                    start = columns[k][j]
                    hold_ref[0, k, j] = start + (0.5 * twelfth) * term[k]
                    acc_ref[k, j] = start + (twelfth / 6.0) * term[k]
                elif stage == 0:
                    adj_ref[one, k, j] = acc_ref[k, j] + (twelfth / 6.0) * term[k]
                else:
                    scale = (0.5 if stage == 2 else 1.0) * twelfth
                    hold_ref[1 if stage == 2 else 0, k, j] = adj_ref[one, k, j] + scale * term[k]
                    acc_ref[k, j] = acc_ref[k, j] + (twelfth / 3.0) * term[k]


def kernel(
    seeds_ref, near_ref, far_ref, blocks_ref, out_ref,
    wide_ref, adj_ref, acc_ref, hold_ref, base_ref, coef_ref, now_ref, flux_ref, slope_ref,
):
    funcs, _, strip, _ = seeds_ref.shape
    spread, _, block, _ = blocks_ref.shape
    tall = strip + 2 * RIM
    depth, base_depth = tall // SUB, (strip + 2 * BASE_RIM) // SUB
    even = lax.rem(lax.axis_index("tile"), 2) == 0

    def lay(left_ref, right_ref, left_part, right_part):
        for one in range(funcs):
            for k in range(FIELDS):
                wide_ref[one, k, :RIM, :] = left_ref[one, k]
                wide_ref[one, k, RIM + strip :, :] = right_ref[one, k]
        for owner in range(spread):
            start = owner * block
            for moment in range(STEPS):
                for k in range(FIELDS):
                    field = moment * FIELDS + k
                    if start >= strip - BASE_RIM:
                        place = start - (strip - BASE_RIM)
                        base_ref[moment, k, place : place + block, :] = blocks_ref[owner, left_part * STEPS * FIELDS + field]
                    if start + block <= BASE_RIM:
                        place = BASE_RIM + strip + start
                        base_ref[moment, k, place : place + block, :] = blocks_ref[owner, right_part * STEPS * FIELDS + field]

    pl.when(even)(lambda: lay(far_ref, near_ref, 2, 1))
    pl.when(jnp.logical_not(even))(lambda: lay(near_ref, far_ref, 1, 2))
    for one in range(funcs):
        for k in range(FIELDS):
            wide_ref[one, k, RIM : RIM + strip, :] = seeds_ref[one, k]
    for owner in range(spread):
        place = BASE_RIM + owner * block
        for moment in range(STEPS):
            for k in range(FIELDS):
                base_ref[moment, k, place : place + block, :] = blocks_ref[owner, moment * FIELDS + k]
    for one in range(funcs):
        for k in range(FIELDS):
            for j in range(depth):
                adj_ref[one, k, j] = wide_ref[one, k, pl.ds(j, SUB, stride=depth), :]

    def one_step(index, carry):
        moment = STEPS - 1 - index
        state_stages(moment, base_ref, coef_ref, now_ref, flux_ref, slope_ref, base_depth)

        def one_func(one, inner):
            pull_stages(one, coef_ref, adj_ref, acc_ref, hold_ref, depth)
            return inner

        return lax.fori_loop(0, funcs, one_func, carry)

    lax.fori_loop(0, STEPS, one_step, 0)
    for one in range(funcs):
        for k in range(FIELDS):
            for j in range(depth):
                wide_ref[one, k, pl.ds(j, SUB, stride=depth), :] = adj_ref[one, k, j]
            out_ref[one, k] = wide_ref[one, k, RIM : RIM + strip, :]


def local(seeds, checkpoints):
    funcs, _, strip, _ = seeds.shape
    block = checkpoints.shape[2]
    even = lax.rem(lax.axis_index("tile"), 2) == 0
    own = checkpoints.reshape(STEPS * FIELDS, block, LANES)
    far_base, near_base = swap_far(own), swap_near(own)
    tail = strip - RIM
    far_edge = lax.dynamic_slice_in_dim(seeds, jnp.where(even, 0, tail), RIM, axis=2)
    near_edge = lax.dynamic_slice_in_dim(seeds, jnp.where(even, tail, 0), RIM, axis=2)
    far, near = swap_far(far_edge), swap_near(near_edge)
    blocks = lax.all_gather(jnp.concatenate([own, near_base, far_base], axis=0), "func", axis=0, tiled=False)
    tall, base_tall = strip + 2 * RIM, strip + 2 * BASE_RIM
    depth, base_depth = tall // SUB, base_tall // SUB
    shapes = [
        (funcs, FIELDS, tall, LANES),
        (funcs, FIELDS, depth, SUB, LANES),
        (FIELDS, depth, SUB, LANES),
        (2, FIELDS, depth, SUB, LANES),
        (STEPS, FIELDS, base_tall, LANES),
        (4, 5, base_tall, LANES),
        (FIELDS, base_depth, SUB, LANES),
        (FIELDS, base_depth, SUB, LANES),
        (FIELDS, base_depth, SUB, LANES),
    ]
    vmem = pl.BlockSpec(memory_space=pltpu.VMEM)
    return pl.pallas_call(
        kernel,
        out_shape=jax.ShapeDtypeStruct(seeds.shape, jnp.float32),
        in_specs=[vmem] * 4,
        out_specs=vmem,
        scratch_shapes=[pltpu.VMEM(shape, jnp.float32) for shape in shapes],
        compiler_params=pltpu.CompilerParams(vmem_limit_bytes=32 * 1024 * 1024),
        name="two_steps",
    )(seeds, near, far, blocks)


def solution(mesh):
    return jax.shard_map(
        local,
        mesh=mesh,
        in_specs=(P("func", None, "tile", None), P(None, None, ("tile", "func"), None)),
        out_specs=P("func", None, "tile", None),
        check_vma=False,
    )
```

time: 92.3 us -> 41.5 us (0.45)
  waiting for transfers between devices: 33.9 us -> 1.05 us
  Pallas kernels: 0 us -> 23.9 us
  starting transfers between devices: 29.1 us -> 8.15 us
  other arithmetic: 8.91 us -> 0.01 us
  local copies, waits for them, and re-layouts: 7.21 us -> 1 us
  blocking collectives: 11.5 us -> 7.15 us
  between operations: 1.52 us -> 0.03 us
    ppermute x20 -> x4, waiting for transfers between devices: 33.9 us -> 1.05 us  [the longest x2 1.05 us: swap_near(): return lax.ppermute(cells, 'tile', [(i, i ^ 1) for i in range(count)])]
    pallas_call x0 -> x1, Pallas kernels: none -> 23.9 us  [local(): pl.pallas_call(kernel, out_shape=jax.ShapeDtypeStruct(seeds.shape, jnp.fl...]
    ppermute x20 -> x4, starting transfers between devices: 29.1 us -> 8.15 us  [the longest x2 7.95 us: swap_far(): return lax.ppermute(cells, 'tile', pairs)]
    slice x67 -> x0, local copies, waits for them, and re-layouts: 7.16 us -> none  [the longest x28 3.15 us: diff_second(): jnp.roll(field, NZ, axis=-1)]
    all_gather x2 -> x1, blocking collectives: 11.5 us -> 7.15 us  [local(): lax.all_gather(jnp.concatenate([own, near_base, far_base], axis=0), 'func...]
    div x16 -> x0, other arithmetic: 3.66 us -> none  [the longest x8 2.59 us: diff_second(): (jnp.roll(field, 2 * NZ, axis=-1) - jnp.roll(field, -2 * NZ, axis=-1) + 8...]
    add x13 -> x0, other arithmetic: 2.9 us -> none  [the longest x1 0.91 us: local(): adjoint = adjoint + term_one + term_two + term_three + term_four]
    add_any x24 -> x0, other arithmetic: 1.13 us -> none  [the longest x16 0.85 us: pressure(): mom_z * mom_z]
  transfers between devices with their start and end apart: 20 -> 4, of which waited for: 15 -> 1; matrix products, arithmetic and copies ran while one was open for 7% -> 2% of each run, Pallas kernels for 0% -> 0%
where the time goes in v1:
time: 41.5 us; the launch traced here: 41.3 us
  Pallas kernels  23.9 us (58%)
  starting transfers between devices  8.15 us (20%)
  blocking collectives  7.15 us (17%)
  waiting for transfers between devices  1.05 us (3%)
  local copies, waits for them, and re-layouts  1 us (2%)
    pallas_call x1, Pallas kernels, local(): pl.pallas_call(kernel, out_shape=jax.ShapeDtypeStruct(seeds.shape, jnp.fl...  23.9 us
    ppermute x2, starting transfers between devices, swap_far(): return lax.ppermute(cells, 'tile', pairs)  7.95 us
    all_gather x1, blocking collectives, local(): lax.all_gather(jnp.concatenate([own, near_base, far_base], axis=0), 'func...  7.15 us
    ppermute x2, waiting for transfers between devices, swap_near(): return lax.ppermute(cells, 'tile', [(i, i ^ 1) for i in range(count)])  1.05 us
    dynamic_slice x1, local copies, waits for them, and re-layouts, local(): lax.dynamic_slice_in_dim(seeds, jnp.where(even, 0, tail), RIM, axis=2)  0.99 us
  transfers between devices with their start and end apart: 4, of which 1 were waited for; matrix products, arithmetic and copies ran while one was open for 2% of the time, Pallas kernels for 0%

profile of v1, /device:TPU:0, one launch (start us, length us, event | category | flops | bytes accessed | tf_op | source)
XLA Modules:
  0.0 41.3 jit_solution(6007446537074976697)
XLA Ops:
  0.0 6.0 %collective-permute-start.3 = (f32[10,8,128]{2,1,0:T(8,128)}, f32[10,8,128]{2,1,0:T(8,128)S(1)}, u32[]{:S(2)}, u32[]{:S(2)}) collective-permute-start(f32[10,8,128]{2,1,0:T(8,128)} %bitcast.3), channel_id=1, source_target_pairs={{0,28},{4,8},{8,4},{12,16},{16,12},{20,24},{24,20},{28,0},{1,29},{... | collective-permute-start | bytes 122888 | tf_op jit(solution)/shard_map/ppermute | solution.py:29
  6.0 0.0 collective-permute-start.2
  6.0 0.0 copy-start.1
  6.0 1.0 %constant_dynamic-slice_fusion = (f32[3,5,16,128]{3,2,1,0:T(8,128)S(1)}, f32[3,5,16,128]{3,2,1,0:T(8,128)S(1)}) fusion(f32[3,5,32,128]{3,2,1,0:T(8,128)} %seeds_ref.1, s32[]{:T(128)S(6)} %select_n.10, s32[]{:T(128)S(6)} %select_n.9), kind=kLoop, calls=%fused_computation.1 | loop fusion | bytes 491528 | tf_op jit(solution)/shard_map/dynamic_slice | solution.py:208
  7.0 2.0 %collective-permute-start.1 = (f32[3,5,16,128]{3,2,1,0:T(8,128)S(1)}, f32[3,5,16,128]{3,2,1,0:T(8,128)S(1)}, u32[]{:S(2)}, u32[]{:S(2)}) collective-permute-start(f32[3,5,16,128]{3,2,1,0:T(8,128)S(1)} %get-tuple-element.5), channel_id=1, source_target_pairs={{0,28},{4,8},{8,4},{12,16},{16,12},{20,24},{24,20},{28,0},{1,29},{... | collective-permute-start | bytes 368648 | tf_op jit(solution)/shard_map/ppermute | solution.py:29
  8.9 0.2 collective-permute-start
  9.1 0.0 collective-permute-done.3
  9.1 1.0 %collective-permute-done.2 = f32[10,8,128]{2,1,0:T(8,128)S(1)} collective-permute-done((f32[10,8,128]{2,1,0:T(8,128)}, f32[10,8,128]{2,1,0:T(8,128)S(1)}, u32[]{:S(2)}, u32[]{:S(2)}) %collective-permute-start.2) | collective-permute-done | bytes 40992 | tf_op jit(solution)/shard_map/ppermute | solution.py:23
  10.2 0.0 copy-done.1
  10.2 0.0 copy-start
  10.2 7.2 %all-gather = f32[120,8,128]{2,1,0:T(8,128)S(1)} all-gather(f32[30,8,128]{2,1,0:T(8,128)S(1)} %pad_maximum_fusion), channel_id=2, replica_groups=mesh['tile'=8,'func'=4] {'func'}, dimensions={0}, use_global_device_ids=true | all-gather | bytes 614400 | tf_op jit(solution)/shard_map/all_gather | solution.py:211
  17.4 0.0 collective-permute-done.1.far_ref
  17.4 0.0 collective-permute-done.near_ref
  17.4 0.0 copy-done
  17.4 23.9 %two_steps.1 = f32[3,5,32,128]{3,2,1,0:T(8,128)} custom-call(f32[3,5,32,128]{3,2,1,0:T(8,128)S(1)} %copy-done, f32[3,5,16,128]{3,2,1,0:T(8,128)S(1)} %collective-permute-done.near_ref, f32[3,5,16,128]{3,2,1,0:T(8,128)S(1)} %collective-permute-done.1.far_ref, f32[4,30,8,128]{3,2,1,0:T(8,128)S(1)} %bitcast.2), custom_call_target="tpu_custom_call" | custom-call | tf_op jit(solution)/shard_map/two_steps/pallas_call | solution.py:226
  (1 shorter events, 0.0 us)
Async XLA Ops:
  0.0 9.1 %collective-permute-start.3 = (f32[10,8,128]{2,1,0:T(8,128)}, f32[10,8,128]{2,1,0:T(8,128)S(1)}, u32[]{:S(2)}, u32[]{:S(2)}) collective-permute-start(f32[10,8,128]{2,1,0:T(8,128)} %bitcast.3), channel_id=1, source_target_pairs={{0,28},{4,8},{8,4},{12,16},{16,12},{20,24},{24,20},{28,0},{1,29},{... | collective-permute-start | bytes 122888 | tf_op jit(solution)/shard_map/ppermute | solution.py:29
  6.0 4.2 %collective-permute-start.2 = (f32[10,8,128]{2,1,0:T(8,128)}, f32[10,8,128]{2,1,0:T(8,128)S(1)}, u32[]{:S(2)}, u32[]{:S(2)}) collective-permute-start(f32[10,8,128]{2,1,0:T(8,128)} %bitcast.4), channel_id=1, source_target_pairs={{0,4},{4,0},{8,12},{12,8},{16,20},{20,16},{24,28},{28,24},{1,5},{5... | collective-permute-start | bytes 122888 | tf_op jit(solution)/shard_map/ppermute | solution.py:23
  6.0 4.2 %copy-start.1 = (f32[2,5,8,128]{3,2,1,0:T(8,128)S(1)}, f32[2,5,8,128]{3,2,1,0:T(8,128)}, u32[]{:S(2)}) copy-start(f32[2,5,8,128]{3,2,1,0:T(8,128)} %param.3) | copy-start | bytes 122884
  7.0 10.4 %collective-permute-start.1 = (f32[3,5,16,128]{3,2,1,0:T(8,128)S(1)}, f32[3,5,16,128]{3,2,1,0:T(8,128)S(1)}, u32[]{:S(2)}, u32[]{:S(2)}) collective-permute-start(f32[3,5,16,128]{3,2,1,0:T(8,128)S(1)} %get-tuple-element.5), channel_id=1, source_target_pairs={{0,28},{4,8},{8,4},{12,16},{16,12},{20,24},{24,20},{28,0},{1,29},{... | collective-permute-start | bytes 368648 | tf_op jit(solution)/shard_map/ppermute | solution.py:29
  8.9 8.4 %collective-permute-start = (f32[3,5,16,128]{3,2,1,0:T(8,128)S(1)}, f32[3,5,16,128]{3,2,1,0:T(8,128)S(1)}, u32[]{:S(2)}, u32[]{:S(2)}) collective-permute-start(f32[3,5,16,128]{3,2,1,0:T(8,128)S(1)} %get-tuple-element.6), channel_id=1, source_target_pairs={{0,4},{4,0},{8,12},{12,8},{16,20},{20,16},{24,28},{28,24},{1,5},{5... | collective-permute-start | bytes 368648 | tf_op jit(solution)/shard_map/ppermute | solution.py:23
  10.2 7.2 %copy-start = (f32[3,5,32,128]{3,2,1,0:T(8,128)S(1)}, f32[3,5,32,128]{3,2,1,0:T(8,128)}, u32[]{:S(2)}) copy-start(f32[3,5,32,128]{3,2,1,0:T(8,128)} %seeds_ref.1) | copy-start | bytes 737284

commit v2 on v1

v2 whole, which is shorter than its diff:
```python
import jax
import jax.numpy as jnp
from jax import lax
from jax.experimental import pallas as pl
from jax.experimental.pallas import tpu as pltpu
from jax.sharding import PartitionSpec as P

NZ = 4
STEPS = 2
FIELDS = 5
LANES = 128
SUB = 8

step_size = 0.3
twelfth = step_size / 12.0

RIM = 16
BASE_RIM = 24


def swap_near(cells):
    count = lax.axis_size("tile")
    return lax.ppermute(cells, "tile", [(i, i ^ 1) for i in range(count)])


def swap_far(cells):
    count = lax.axis_size("tile")
    pairs = [(i, (i + (1 if i % 2 else -1)) % count) for i in range(count)]
    return lax.ppermute(cells, "tile", pairs)


def turn(cells, places, axis):
    return pltpu.roll(cells, places % cells.shape[axis], axis)


def second_weights():
    shape = (LANES, LANES)
    ahead = lax.broadcasted_iota(jnp.int32, shape, 0) - lax.broadcasted_iota(jnp.int32, shape, 1)
    ahead = jnp.bitwise_and(ahead, LANES - 1)
    weights = jnp.zeros(shape, jnp.float32)
    for places, weight in ((NZ, 8.0), (-NZ, -8.0), (2 * NZ, -1.0), (-2 * NZ, 1.0)):
        weights = jnp.where(ahead == places % LANES, weight, weights)
    return jnp.concatenate([weights, weights], axis=0).astype(jnp.bfloat16)


def diff_second(cells, weights):
    high = cells.astype(jnp.bfloat16)
    low = (cells - high.astype(jnp.float32)).astype(jnp.bfloat16)
    return jnp.dot(jnp.concatenate([high, low], axis=1), weights, preferred_element_type=jnp.float32)


def diff_first(back_two, back_one, next_one, next_two):
    return 8.0 * (next_one - back_one) - (next_two - back_two)


class Column:
    def __init__(self, load, depth):
        self.load, self.depth, self.held = load, depth, {}

    def __getitem__(self, place):
        if place not in self.held:
            if place < 0:
                cells = turn(self[place + self.depth], 1, 0)
            elif place >= self.depth:
                cells = turn(self[place - self.depth], -1, 0)
            else:
                cells = self.load(place)
            self.held[place] = cells
        return self.held[place]

    def diff(self, place):
        return diff_first(self[place - 2], self[place - 1], self[place + 1], self[place + 2])


def primitives(state):
    density, mom_x, mom_y, mom_z, energy = state
    inverse = 1.0 / density
    vel_x, vel_y, vel_z = mom_x * inverse, mom_y * inverse, mom_z * inverse
    half = 0.5 * (vel_x * vel_x + vel_y * vel_y + vel_z * vel_z)
    press = 0.4 * (energy - density * half)
    total = energy + press
    return vel_x, vel_y, vel_z, total * inverse, half, press, total


def tile(place):
    return slice(place * SUB, (place + 1) * SUB)


def state_stages(base_ref, coef_ref, now_ref, flux_ref, slope_ref, weights, depth):
    tall = depth * SUB

    def rows(place):
        return pl.ds(place, SUB, stride=depth)

    for stage in range(4):
        for moment in range(STEPS):
            for j in range(depth):
                if stage == 0:
                    state = [base_ref[moment, k, rows(j), :] for k in range(FIELDS)]
                else:
                    state = [now_ref[moment, k, tile(j)] for k in range(FIELDS)]
                vel_x, vel_y, vel_z, heat, half, press, total = primitives(state)
                for k, cells in enumerate((vel_x, vel_y, vel_z, heat, half)):
                    coef_ref[moment, stage, k, rows(j), :] = cells
                if stage == 3:
                    continue
                _, mom_x, mom_y, mom_z, _ = state
                cross = mom_x * vel_y
                first = (mom_x, mom_x * vel_x + press, cross, mom_z * vel_x, total * vel_x)
                second = (mom_y, cross, mom_y * vel_y + press, mom_z * vel_y, total * vel_y)
                for k in range(FIELDS):
                    flux_ref[moment, k, tile(j)] = first[k]
                    slope_ref[moment, k, tile(j)] = second[k]
            if stage == 3:
                continue
            second = diff_second(slope_ref[moment].reshape(FIELDS * tall, LANES), weights)
            slope_ref[moment] = second.reshape(FIELDS, tall, LANES)
        if stage == 3:
            return
        scale = (0.5 if stage < 2 else 1.0) * twelfth
        for moment in range(STEPS):
            for k in range(FIELDS):
                column = Column(lambda place, k=k: flux_ref[moment, k, tile(place)], depth)
                for j in range(depth):
                    slope = column.diff(j) + slope_ref[moment, k, tile(j)]
                    now_ref[moment, k, tile(j)] = base_ref[moment, k, rows(j), :] - scale * slope


def pull_stages(moment, coef_ref, adj_ref, acc_ref, hold_ref, second_ref, weights, depth):
    shift = BASE_RIM - RIM
    funcs, tall = adj_ref.shape[0], depth * SUB
    for stage in (3, 2, 1, 0):
        source_ref = (adj_ref, hold_ref.at[0], hold_ref.at[1], hold_ref.at[0])[3 - stage]

        def second_of(one):
            second = diff_second(source_ref[one].reshape(FIELDS * tall, LANES), weights)
            second_ref[one] = second.reshape(FIELDS, tall, LANES)

        second_of(0)
        for one in range(funcs):
            if one + 1 < funcs:
                second_of(one + 1)
            columns = [Column(lambda place, k=k: source_ref[one, k, tile(place)], depth) for k in range(FIELDS)]
            for j in range(depth):
                vel_x, vel_y, vel_z, heat, half = [
                    coef_ref[moment, stage, k, pl.ds(shift + j, SUB, stride=depth), :] for k in range(5)
                ]
                a = [column.diff(j) for column in columns]
                b = [second_ref[one, k, tile(j)] for k in range(FIELDS)]
                mix_x = vel_x * a[1] + vel_y * a[2] + vel_z * a[3] + heat * a[4]
                mix_y = vel_x * b[1] + vel_y * b[2] + vel_z * b[3] + heat * b[4]
                lift = vel_x * a[4] + vel_y * b[4]
                press = 0.4 * (a[1] + b[2] + lift)
                term = (
                    half * press - vel_x * mix_x - vel_y * mix_y,
                    a[0] + mix_x + vel_x * (a[1] - press) + vel_y * b[1],
                    b[0] + mix_y + vel_y * (b[2] - press) + vel_x * a[2],
                    vel_x * a[3] + vel_y * b[3] - vel_z * press,
                    lift + press,
                )
                for k in range(FIELDS):
                    if stage == 3:
                        start = columns[k][j]
                        hold_ref[0, one, k, tile(j)] = start + (0.5 * twelfth) * term[k]
                        acc_ref[one, k, tile(j)] = start + (twelfth / 6.0) * term[k]
                    elif stage == 0:
                        adj_ref[one, k, tile(j)] = acc_ref[one, k, tile(j)] + (twelfth / 6.0) * term[k]
                    else:
                        scale = (0.5 if stage == 2 else 1.0) * twelfth
                        place = 1 if stage == 2 else 0
                        hold_ref[place, one, k, tile(j)] = adj_ref[one, k, tile(j)] + scale * term[k]
                        acc_ref[one, k, tile(j)] = acc_ref[one, k, tile(j)] + (twelfth / 3.0) * term[k]


def kernel(
    seeds_ref, near_ref, far_ref, blocks_ref, out_ref,
    wide_ref, adj_ref, acc_ref, hold_ref, second_ref, base_ref, coef_ref, now_ref, flux_ref, slope_ref,
):
    funcs, _, strip, _ = seeds_ref.shape
    spread, _, block, _ = blocks_ref.shape
    tall = strip + 2 * RIM
    depth, base_depth = tall // SUB, (strip + 2 * BASE_RIM) // SUB
    even = lax.rem(lax.axis_index("tile"), 2) == 0

    def lay(left_ref, right_ref, left_part, right_part):
        for one in range(funcs):
            for k in range(FIELDS):
                wide_ref[one, k, :RIM, :] = left_ref[one, k]
                wide_ref[one, k, RIM + strip :, :] = right_ref[one, k]
        for owner in range(spread):
            start = owner * block
            for moment in range(STEPS):
                for k in range(FIELDS):
                    field = moment * FIELDS + k
                    if start >= strip - BASE_RIM:
                        place = start - (strip - BASE_RIM)
                        base_ref[moment, k, place : place + block, :] = blocks_ref[owner, left_part * STEPS * FIELDS + field]
                    if start + block <= BASE_RIM:
                        place = BASE_RIM + strip + start
                        base_ref[moment, k, place : place + block, :] = blocks_ref[owner, right_part * STEPS * FIELDS + field]

    pl.when(even)(lambda: lay(far_ref, near_ref, 2, 1))
    pl.when(jnp.logical_not(even))(lambda: lay(near_ref, far_ref, 1, 2))
    for one in range(funcs):
        for k in range(FIELDS):
            wide_ref[one, k, RIM : RIM + strip, :] = seeds_ref[one, k]
    for owner in range(spread):
        place = BASE_RIM + owner * block
        for moment in range(STEPS):
            for k in range(FIELDS):
                base_ref[moment, k, place : place + block, :] = blocks_ref[owner, moment * FIELDS + k]
    for one in range(funcs):
        for k in range(FIELDS):
            for j in range(depth):
                adj_ref[one, k, tile(j)] = wide_ref[one, k, pl.ds(j, SUB, stride=depth), :]

    weights = second_weights()
    state_stages(base_ref, coef_ref, now_ref, flux_ref, slope_ref, weights, base_depth)

    def one_step(index, carry):
        moment = STEPS - 1 - index
        pull_stages(moment, coef_ref, adj_ref, acc_ref, hold_ref, second_ref, weights, depth)
        return carry

    lax.fori_loop(0, STEPS, one_step, 0)
    for one in range(funcs):
        for k in range(FIELDS):
            for j in range(depth):
                wide_ref[one, k, pl.ds(j, SUB, stride=depth), :] = adj_ref[one, k, tile(j)]
            out_ref[one, k] = wide_ref[one, k, RIM : RIM + strip, :]


def local(seeds, checkpoints):
    funcs, _, strip, _ = seeds.shape
    block = checkpoints.shape[2]
    even = lax.rem(lax.axis_index("tile"), 2) == 0
    own = checkpoints.reshape(STEPS * FIELDS, block, LANES)
    far_base, near_base = swap_far(own), swap_near(own)
    tail = strip - RIM
    far_edge = lax.dynamic_slice_in_dim(seeds, jnp.where(even, 0, tail), RIM, axis=2)
    near_edge = lax.dynamic_slice_in_dim(seeds, jnp.where(even, tail, 0), RIM, axis=2)
    far, near = swap_far(far_edge), swap_near(near_edge)
    blocks = lax.all_gather(jnp.concatenate([own, near_base, far_base], axis=0), "func", axis=0, tiled=False)
    tall, base_tall = strip + 2 * RIM, strip + 2 * BASE_RIM
    shapes = [
        (funcs, FIELDS, tall, LANES),
        (funcs, FIELDS, tall, LANES),
        (funcs, FIELDS, tall, LANES),
        (2, funcs, FIELDS, tall, LANES),
        (funcs, FIELDS, tall, LANES),
        (STEPS, FIELDS, base_tall, LANES),
        (STEPS, 4, 5, base_tall, LANES),
        (STEPS, FIELDS, base_tall, LANES),
        (STEPS, FIELDS, base_tall, LANES),
        (STEPS, FIELDS, base_tall, LANES),
    ]
    vmem = pl.BlockSpec(memory_space=pltpu.VMEM)
    return pl.pallas_call(
        kernel,
        out_shape=jax.ShapeDtypeStruct(seeds.shape, jnp.float32),
        in_specs=[vmem] * 4,
        out_specs=vmem,
        scratch_shapes=[pltpu.VMEM(shape, jnp.float32) for shape in shapes],
        compiler_params=pltpu.CompilerParams(vmem_limit_bytes=32 * 1024 * 1024),
        name="two_steps",
    )(seeds, near, far, blocks)


def solution(mesh):
    return jax.shard_map(
        local,
        mesh=mesh,
        in_specs=(P("func", None, "tile", None), P(None, None, ("tile", "func"), None)),
        out_specs=P("func", None, "tile", None),
        check_vma=False,
    )
```

time: 41.5 us -> 22.6 us (0.54)
  Pallas kernels: 23.9 us -> 5.03 us
    pallas_call x1, Pallas kernels: 23.9 us -> 5.03 us  [local(): pl.pallas_call(kernel, out_shape=jax.ShapeDtypeStruct(seeds.shape, jnp.fl...]
  transfers between devices with their start and end apart: 4 -> 4, of which waited for: 1 -> 1; matrix products, arithmetic and copies ran while one was open for 2% -> 4% of each run, Pallas kernels for 0% -> 0%
where the time goes in v2:
time: 22.6 us; the launch traced here: 22.4 us
  starting transfers between devices  8.15 us (36%)
  blocking collectives  7.15 us (32%)
  Pallas kernels  5.03 us (22%)
  waiting for transfers between devices  1.05 us (5%)
  local copies, waits for them, and re-layouts  1 us (4%)
    ppermute x2, starting transfers between devices, swap_far(): return lax.ppermute(cells, 'tile', pairs)  7.95 us
    all_gather x1, blocking collectives, local(): lax.all_gather(jnp.concatenate([own, near_base, far_base], axis=0), 'func...  7.15 us
    pallas_call x1, Pallas kernels, local(): pl.pallas_call(kernel, out_shape=jax.ShapeDtypeStruct(seeds.shape, jnp.fl...  5.03 us
    ppermute x2, waiting for transfers between devices, swap_near(): return lax.ppermute(cells, 'tile', [(i, i ^ 1) for i in range(count)])  1.05 us
    dynamic_slice x1, local copies, waits for them, and re-layouts, local(): lax.dynamic_slice_in_dim(seeds, jnp.where(even, 0, tail), RIM, axis=2)  0.99 us
  transfers between devices with their start and end apart: 4, of which 1 were waited for; matrix products, arithmetic and copies ran while one was open for 4% of the time, Pallas kernels for 0%

profile of v2, /device:TPU:0, one launch (start us, length us, event | category | flops | bytes accessed | tf_op | source)
XLA Modules:
  0.0 22.4 jit_solution(18052724292919439073)
XLA Ops:
  0.0 6.0 %collective-permute-start.3 = (f32[10,8,128]{2,1,0:T(8,128)}, f32[10,8,128]{2,1,0:T(8,128)S(1)}, u32[]{:S(2)}, u32[]{:S(2)}) collective-permute-start(f32[10,8,128]{2,1,0:T(8,128)} %bitcast.3), channel_id=1, source_target_pairs={{0,28},{4,8},{8,4},{12,16},{16,12},{20,24},{24,20},{28,0},{1,29},{... | collective-permute-start | bytes 122888 | tf_op jit(solution)/shard_map/ppermute | solution.py:29
  6.0 0.0 collective-permute-start.2
  6.0 0.0 copy-start.1
  6.0 1.0 %constant_dynamic-slice_fusion = (f32[3,5,16,128]{3,2,1,0:T(8,128)S(1)}, f32[3,5,16,128]{3,2,1,0:T(8,128)S(1)}) fusion(f32[3,5,32,128]{3,2,1,0:T(8,128)} %seeds_ref.1, s32[]{:T(128)S(6)} %select_n.10, s32[]{:T(128)S(6)} %select_n.9), kind=kLoop, calls=%fused_computation.1 | loop fusion | bytes 491528 | tf_op jit(solution)/shard_map/dynamic_slice | solution.py:240
  7.0 2.0 %collective-permute-start.1 = (f32[3,5,16,128]{3,2,1,0:T(8,128)S(1)}, f32[3,5,16,128]{3,2,1,0:T(8,128)S(1)}, u32[]{:S(2)}, u32[]{:S(2)}) collective-permute-start(f32[3,5,16,128]{3,2,1,0:T(8,128)S(1)} %get-tuple-element.5), channel_id=1, source_target_pairs={{0,28},{4,8},{8,4},{12,16},{16,12},{20,24},{24,20},{28,0},{1,29},{... | collective-permute-start | bytes 368648 | tf_op jit(solution)/shard_map/ppermute | solution.py:29
  8.9 0.2 collective-permute-start
  9.1 0.0 collective-permute-done.3
  9.1 1.0 %collective-permute-done.2 = f32[10,8,128]{2,1,0:T(8,128)S(1)} collective-permute-done((f32[10,8,128]{2,1,0:T(8,128)}, f32[10,8,128]{2,1,0:T(8,128)S(1)}, u32[]{:S(2)}, u32[]{:S(2)}) %collective-permute-start.2) | collective-permute-done | bytes 40992 | tf_op jit(solution)/shard_map/ppermute | solution.py:23
  10.2 0.0 copy-done.1
  10.2 0.0 copy-start
  10.2 7.2 %all-gather = f32[120,8,128]{2,1,0:T(8,128)S(1)} all-gather(f32[30,8,128]{2,1,0:T(8,128)S(1)} %pad_maximum_fusion), channel_id=2, replica_groups=mesh['tile'=8,'func'=4] {'func'}, dimensions={0}, use_global_device_ids=true | all-gather | bytes 614400 | tf_op jit(solution)/shard_map/all_gather | solution.py:243
  17.4 0.0 collective-permute-done.1.far_ref
  17.4 0.0 collective-permute-done.near_ref
  17.4 0.0 copy-done
  17.4 5.0 %two_steps.1 = f32[3,5,32,128]{3,2,1,0:T(8,128)} custom-call(f32[3,5,32,128]{3,2,1,0:T(8,128)S(1)} %copy-done, f32[3,5,16,128]{3,2,1,0:T(8,128)S(1)} %collective-permute-done.near_ref, f32[3,5,16,128]{3,2,1,0:T(8,128)S(1)} %collective-permute-done.1.far_ref, f32[4,30,8,128]{3,2,1,0:T(8,128)S(1)} %bitcast.2), custom_call_target="tpu_custom_call" | custom-call | tf_op jit(solution)/shard_map/two_steps/pallas_call | solution.py:258
  (1 shorter events, 0.0 us)
Async XLA Ops:
  0.0 9.1 %collective-permute-start.3 = (f32[10,8,128]{2,1,0:T(8,128)}, f32[10,8,128]{2,1,0:T(8,128)S(1)}, u32[]{:S(2)}, u32[]{:S(2)}) collective-permute-start(f32[10,8,128]{2,1,0:T(8,128)} %bitcast.3), channel_id=1, source_target_pairs={{0,28},{4,8},{8,4},{12,16},{16,12},{20,24},{24,20},{28,0},{1,29},{... | collective-permute-start | bytes 122888 | tf_op jit(solution)/shard_map/ppermute | solution.py:29
  6.0 4.2 %collective-permute-start.2 = (f32[10,8,128]{2,1,0:T(8,128)}, f32[10,8,128]{2,1,0:T(8,128)S(1)}, u32[]{:S(2)}, u32[]{:S(2)}) collective-permute-start(f32[10,8,128]{2,1,0:T(8,128)} %bitcast.4), channel_id=1, source_target_pairs={{0,4},{4,0},{8,12},{12,8},{16,20},{20,16},{24,28},{28,24},{1,5},{5... | collective-permute-start | bytes 122888 | tf_op jit(solution)/shard_map/ppermute | solution.py:23
  6.0 4.2 %copy-start.1 = (f32[2,5,8,128]{3,2,1,0:T(8,128)S(1)}, f32[2,5,8,128]{3,2,1,0:T(8,128)}, u32[]{:S(2)}) copy-start(f32[2,5,8,128]{3,2,1,0:T(8,128)} %param.3) | copy-start | bytes 122884
  7.0 10.4 %collective-permute-start.1 = (f32[3,5,16,128]{3,2,1,0:T(8,128)S(1)}, f32[3,5,16,128]{3,2,1,0:T(8,128)S(1)}, u32[]{:S(2)}, u32[]{:S(2)}) collective-permute-start(f32[3,5,16,128]{3,2,1,0:T(8,128)S(1)} %get-tuple-element.5), channel_id=1, source_target_pairs={{0,28},{4,8},{8,4},{12,16},{16,12},{20,24},{24,20},{28,0},{1,29},{... | collective-permute-start | bytes 368648 | tf_op jit(solution)/shard_map/ppermute | solution.py:29
  8.9 8.4 %collective-permute-start = (f32[3,5,16,128]{3,2,1,0:T(8,128)S(1)}, f32[3,5,16,128]{3,2,1,0:T(8,128)S(1)}, u32[]{:S(2)}, u32[]{:S(2)}) collective-permute-start(f32[3,5,16,128]{3,2,1,0:T(8,128)S(1)} %get-tuple-element.6), channel_id=1, source_target_pairs={{0,4},{4,0},{8,12},{12,8},{16,20},{20,16},{24,28},{28,24},{1,5},{5... | collective-permute-start | bytes 368648 | tf_op jit(solution)/shard_map/ppermute | solution.py:23
  10.2 7.2 %copy-start = (f32[3,5,32,128]{3,2,1,0:T(8,128)S(1)}, f32[3,5,32,128]{3,2,1,0:T(8,128)}, u32[]{:S(2)}) copy-start(f32[3,5,32,128]{3,2,1,0:T(8,128)} %seeds_ref.1) | copy-start | bytes 737284

commit v3 on v2

v3 whole, which is shorter than its diff:
```python
import jax
import jax.numpy as jnp
from jax import lax
from jax.experimental import pallas as pl
from jax.experimental.pallas import tpu as pltpu
from jax.sharding import PartitionSpec as P

NZ = 4
STEPS = 2
FIELDS = 5
LANES = 128
SUB = 8

step_size = 0.3
twelfth = step_size / 12.0

RIM = 16
BASE_RIM = 24
LONG_RIM = 20
SHORT_RIM = 12
STATE_RIMS = (SHORT_RIM, LONG_RIM)
STILL = (1.0, 0.0, 0.0, 0.0, 2.5)
STATE_EDGES = ((8, 8, 16, 16), (0, 0, 8, 8))


def swap_near(cells):
    count = lax.axis_size("tile")
    return lax.ppermute(cells, "tile", [(i, i ^ 1) for i in range(count)])


def swap_far(cells):
    count = lax.axis_size("tile")
    pairs = [(i, (i + (1 if i % 2 else -1)) % count) for i in range(count)]
    return lax.ppermute(cells, "tile", pairs)


def second_weights():
    shape = (LANES, LANES)
    ahead = lax.broadcasted_iota(jnp.int32, shape, 0) - lax.broadcasted_iota(jnp.int32, shape, 1)
    ahead = jnp.bitwise_and(ahead, LANES - 1)
    weights = jnp.zeros(shape, jnp.float32)
    for places, weight in ((NZ, 8.0), (-NZ, -8.0), (2 * NZ, -1.0), (-2 * NZ, 1.0)):
        weights = jnp.where(ahead == places % LANES, weight, weights)
    return jnp.concatenate([weights, weights], axis=0).astype(jnp.bfloat16)


def first_weights(count, total, skip):
    shape = (count, 2 * total)
    column = lax.broadcasted_iota(jnp.int32, shape, 1)
    column = jnp.where(column < total, column, column - total)
    ahead = column - lax.broadcasted_iota(jnp.int32, shape, 0) - skip
    weights = jnp.zeros(shape, jnp.float32)
    for places, weight in ((1, 8.0), (-1, -8.0), (2, -1.0), (-2, 1.0)):
        weights = jnp.where(ahead == places, weight, weights)
    return weights.astype(jnp.bfloat16)


def parts(cells):
    high = cells.astype(jnp.bfloat16)
    return high, (cells - high.astype(jnp.float32)).astype(jnp.bfloat16)


def second_diff(high, low, weights):
    fields, count, _ = high.shape
    cells = jnp.concatenate([high, low], axis=2).reshape(fields * count, 2 * LANES)
    return jnp.dot(cells, weights, preferred_element_type=jnp.float32)


def first_diff(high, low, weights):
    cells = jnp.concatenate([high, low], axis=1)
    cells = jnp.concatenate([cells[k] for k in range(FIELDS)], axis=1)
    return jnp.dot(weights, cells, preferred_element_type=jnp.float32)


def lanes(k):
    return slice(k * LANES, (k + 1) * LANES)


def primitives(state):
    density, mom_x, mom_y, mom_z, energy = state
    inverse = 1.0 / density
    vel_x, vel_y, vel_z = mom_x * inverse, mom_y * inverse, mom_z * inverse
    half = 0.5 * (vel_x * vel_x + vel_y * vel_y + vel_z * vel_z)
    press = 0.4 * (energy - density * half)
    total = energy + press
    return vel_x, vel_y, vel_z, total * inverse, half, press, total


def tiles(start, stop):
    return [slice(place, place + SUB) for place in range(start, stop, SUB)]


def within(cells, rows, edge, span, k):
    if edge <= rows.start and rows.stop <= span - edge:
        return cells
    place = rows.start + lax.broadcasted_iota(jnp.int32, cells.shape, 0)
    return jnp.where(jnp.logical_and(place >= edge, place < span - edge), cells, STILL[k])


def state_stages(base_ref, coef_ref, now_ref, flux_ref, slope_ref, first_ref, second_ref, lefts, weights, span):
    for stage in range(4):
        for moment in range(STEPS):
            here, there = STATE_EDGES[moment][stage], STATE_EDGES[moment][min(stage + 1, 3)]
            for rows in tiles(here, span - here):
                source_ref = base_ref if stage == 0 else now_ref
                state = [source_ref[moment, k, rows] for k in range(FIELDS)]
                vel_x, vel_y, vel_z, heat, half, press, total = primitives(state)
                for k, cells in enumerate((vel_x, vel_y, vel_z, heat, half)):
                    coef_ref[moment, stage, k, rows] = cells
                if stage == 3:
                    continue
                _, mom_x, mom_y, mom_z, _ = state
                cross = mom_x * vel_y
                first = (mom_x, mom_x * vel_x + press, cross, mom_z * vel_x, total * vel_x)
                second = (mom_y, cross, mom_y * vel_y + press, mom_z * vel_y, total * vel_y)
                for k in range(FIELDS):
                    flux_ref[moment, k, rows] = first[k]
                    if there <= rows.start < span - there:
                        slope_ref[moment, k, rows] = second[k]
            if stage == 3:
                continue
            count, total_rows = span - 2 * there, span - 2 * here
            left = lefts[count, total_rows]
            flux = flux_ref[moment, :, here : span - here]
            first_ref[moment, there : span - there] = first_diff(*parts(flux), left)
            slope = slope_ref[moment, :, there : span - there]
            second = second_diff(*parts(slope), weights)
            second_ref[moment, :, there : span - there] = second.reshape(FIELDS, count, LANES)
        if stage == 3:
            return
        scale = (0.5 if stage < 2 else 1.0) * twelfth
        for moment in range(STEPS):
            there = STATE_EDGES[moment][stage + 1]
            for k in range(FIELDS):
                for rows in tiles(there, span - there):
                    slope = first_ref[moment, rows, lanes(k)] + second_ref[moment, k, rows]
                    cells = base_ref[moment, k, rows] - scale * slope
                    now_ref[moment, k, rows] = within(cells, rows, BASE_RIM - STATE_RIMS[moment] + 2 * (stage + 1), span, k)


def pull_stages(moment, coef_ref, adj_ref, hold_ref, first_ref, second_ref, out_ref, lefts, weights):
    funcs, _, tall, _ = adj_ref.shape
    shift, last = BASE_RIM - RIM, moment == 0
    start = (STEPS - 1 - moment) * SUB
    for stage in (3, 2, 1, 0):
        edge = start + SUB if stage == 0 else start
        source_ref = adj_ref if stage == 3 else hold_ref.at[2 - stage]
        total = tall - 2 * start
        left = lefts[tall - 2 * edge, total]

        def differences(one):
            high, low = parts(source_ref[one, :, start : tall - start])
            first_ref[one, edge : tall - edge] = first_diff(high, low, left)
            second = second_diff(high, low, weights)
            second_ref[one, :, start : tall - start] = second.reshape(FIELDS, total, LANES)

        differences(0)
        for one in range(funcs):
            if one + 1 < funcs:
                differences(one + 1)
            for rows in tiles(edge, tall - edge):
                base_rows = slice(rows.start + shift, rows.stop + shift)
                vel_x, vel_y, vel_z, heat, half = [coef_ref[moment, stage, k, base_rows] for k in range(5)]
                a = [first_ref[one, rows, lanes(k)] for k in range(FIELDS)]
                b = [second_ref[one, k, rows] for k in range(FIELDS)]
                mix_x = vel_x * a[1] + vel_y * a[2] + vel_z * a[3] + heat * a[4]
                mix_y = vel_x * b[1] + vel_y * b[2] + vel_z * b[3] + heat * b[4]
                lift = vel_x * a[4] + vel_y * b[4]
                press = 0.4 * (a[1] + b[2] + lift)
                term = (
                    half * press - vel_x * mix_x - vel_y * mix_y,
                    a[0] + mix_x + vel_x * (a[1] - press) + vel_y * b[1],
                    b[0] + mix_y + vel_y * (b[2] - press) + vel_x * a[2],
                    vel_x * a[3] + vel_y * b[3] - vel_z * press,
                    lift + press,
                )
                for k in range(FIELDS):
                    adj = adj_ref[one, k, rows]
                    if stage > 0:
                        scale = (1.0 if stage == 1 else 0.5) * twelfth
                        hold_ref[3 - stage, one, k, rows] = adj + scale * term[k]
                        continue
                    one_third, two_thirds, rest = [hold_ref[place, one, k, rows] for place in range(3)]
                    mean = (one_third - adj + rest + 2.0 * two_thirds) * (1.0 / 3.0)
                    result = mean + (twelfth / 6.0) * term[k]
                    if last:
                        out_ref[one, k, rows.start - RIM : rows.stop - RIM] = result
                    else:
                        adj_ref[one, k, rows] = result


def kernel(
    seeds_ref, near_ref, far_ref, blocks_ref, out_ref,
    adj_ref, hold_ref, first_ref, second_ref,
    base_ref, coef_ref, now_ref, flux_ref, slope_ref, base_first_ref, base_second_ref,
):
    funcs, _, strip, _ = seeds_ref.shape
    spread, _, block, _ = blocks_ref.shape
    tall, span = strip + 2 * RIM, strip + 2 * BASE_RIM
    even = lax.rem(lax.axis_index("tile"), 2) == 0

    def lay(left_ref, right_ref):
        for one in range(funcs):
            for k in range(FIELDS):
                adj_ref[one, k, :RIM] = left_ref[one, k]
                adj_ref[one, k, RIM + strip :] = right_ref[one, k]

    def lay_base(part, moment, shift, low, high):
        for owner in range(spread):
            start, stop = max(low, owner * block), min(high, (owner + 1) * block)
            if start < stop:
                rows = slice(start - owner * block, stop - owner * block)
                place = BASE_RIM + shift + start
                for k in range(FIELDS):
                    base_ref[moment, k, place : place + stop - start, :] = blocks_ref[owner, part * FIELDS + k, rows, :]

    for moment in range(STEPS):
        edge = BASE_RIM - STATE_RIMS[moment]
        for start in (STATE_EDGES[moment][0], span - STATE_EDGES[moment][0] - SUB):
            if start < edge or start + SUB > span - edge:
                for k in range(FIELDS):
                    base_ref[moment, k, start : start + SUB] = jnp.full((SUB, LANES), STILL[k], jnp.float32)
    middle = strip // 2
    lay_base(0, 0, 0, 0, strip)
    lay_base(1, 1, 0, 0, strip)
    lay_base(2, 1, strip, 0, middle)
    lay_base(2, 1, -strip, middle, strip)
    lay_base(3, 0, strip, 0, SHORT_RIM)
    lay_base(3, 1, -strip, max(SHORT_RIM, strip - LONG_RIM), middle)
    lay_base(3, 1, strip, middle, min(LONG_RIM, strip - SHORT_RIM))
    lay_base(3, 0, -strip, strip - SHORT_RIM, strip)

    weights = second_weights()
    sizes = {(tall - 2 * start, tall - 2 * start) for start in range(0, STEPS * SUB, SUB)}
    sizes |= {(tall - 2 * start - 2 * SUB, tall - 2 * start) for start in range(0, STEPS * SUB, SUB)}
    for edges in STATE_EDGES:
        sizes |= {(span - 2 * edges[n + 1], span - 2 * edges[n]) for n in range(3)}
    lefts = {size: first_weights(*size, (size[1] - size[0]) // 2) for size in sorted(sizes)}
    state_stages(
        base_ref, coef_ref, now_ref, flux_ref, slope_ref, base_first_ref, base_second_ref, lefts, weights, span
    )
    pl.when(even)(lambda: lay(far_ref, near_ref))
    pl.when(jnp.logical_not(even))(lambda: lay(near_ref, far_ref))
    for one in range(funcs):
        for k in range(FIELDS):
            adj_ref[one, k, RIM : RIM + strip] = seeds_ref[one, k]
    for moment in reversed(range(STEPS)):
        pull_stages(moment, coef_ref, adj_ref, hold_ref, first_ref, second_ref, out_ref, lefts, weights)


def local(seeds, checkpoints):
    funcs, _, strip, _ = seeds.shape
    block = checkpoints.shape[2]
    even = lax.rem(lax.axis_index("tile"), 2) == 0
    far_base, near_base = swap_far(checkpoints), swap_near(checkpoints)
    tail = strip - RIM
    far_edge = lax.dynamic_slice_in_dim(seeds, jnp.where(even, 0, tail), RIM, axis=2)
    near_edge = lax.dynamic_slice_in_dim(seeds, jnp.where(even, tail, 0), RIM, axis=2)
    far, near = swap_far(far_edge), swap_near(near_edge)
    lower = lax.axis_index("func") * block < strip // 2
    take_far = even != lower
    main = lax.select(take_far, far_base, near_base)
    other = lax.select(take_far, near_base[1], far_base[1])
    place = lax.axis_index("func") * block + lax.broadcasted_iota(jnp.int32, (1, block, 1), 1)
    inner = jnp.logical_and(place >= SHORT_RIM, place < strip - SHORT_RIM)
    rest = jnp.where(inner, other, main[0])
    own = checkpoints.reshape(STEPS * FIELDS, block, LANES)
    packed = jnp.concatenate([own, main[1], rest], axis=0)
    blocks = lax.all_gather(packed, "func", axis=0, tiled=False)
    tall, span = strip + 2 * RIM, strip + 2 * BASE_RIM
    shapes = [
        (funcs, FIELDS, tall, LANES),
        (3, funcs, FIELDS, tall, LANES),
        (funcs, tall, FIELDS * LANES),
        (funcs, FIELDS, tall, LANES),
        (STEPS, FIELDS, span, LANES),
        (STEPS, 4, 5, span, LANES),
        (STEPS, FIELDS, span, LANES),
        (STEPS, FIELDS, span, LANES),
        (STEPS, FIELDS, span, LANES),
        (STEPS, span, FIELDS * LANES),
        (STEPS, FIELDS, span, LANES),
    ]
    vmem = pl.BlockSpec(memory_space=pltpu.VMEM)
    return pl.pallas_call(
        kernel,
        out_shape=jax.ShapeDtypeStruct(seeds.shape, jnp.float32),
        in_specs=[vmem] * 4,
        out_specs=vmem,
        scratch_shapes=[pltpu.VMEM(shape, jnp.float32) for shape in shapes],
        compiler_params=pltpu.CompilerParams(vmem_limit_bytes=32 * 1024 * 1024),
        name="two_steps",
    )(seeds, near, far, blocks)


def solution(mesh):
    return jax.shard_map(
        local,
        mesh=mesh,
        in_specs=(P("func", None, "tile", None), P(None, None, ("tile", "func"), None)),
        out_specs=P("func", None, "tile", None),
        check_vma=False,
    )
```

time: 22.6 us -> 21.4 us (0.947)
  blocking collectives: 7.15 us -> 6.26 us
  Pallas kernels: 5.03 us -> 4.29 us
  local copies, waits for them, and re-layouts: 1 us -> 1.69 us
  starting transfers between devices: 8.15 us -> 7.73 us
    ppermute x2, starting transfers between devices: 7.95 us -> 4.79 us  [swap_far(): return lax.ppermute(cells, 'tile', pairs)]
    ppermute x2, starting transfers between devices: 0.2 us -> 2.94 us  [swap_near(): return lax.ppermute(cells, 'tile', [(i, i ^ 1) for i in range(count)])]
    ppermute x2, waiting for transfers between devices: 0.01 us -> 1.11 us  [swap_far(): return lax.ppermute(cells, 'tile', pairs)]
    ppermute x2, waiting for transfers between devices: 1.05 us -> 0.01 us  [swap_near(): return lax.ppermute(cells, 'tile', [(i, i ^ 1) for i in range(count)])]
    all_gather x1, blocking collectives: 7.15 us -> 6.26 us  [local(): blocks = lax.all_gather(packed, 'func', axis=0, tiled=False)]
    pallas_call x1, Pallas kernels: 5.03 us -> 4.29 us  [local(): pl.pallas_call(kernel, out_shape=jax.ShapeDtypeStruct(seeds.shape, jnp.fl...]
    unnamed x4, local copies, waits for them, and re-layouts: 0.01 us -> 0.7 us
  transfers between devices with their start and end apart: 4 -> 4, of which waited for: 1 -> 1; matrix products, arithmetic and copies ran while one was open for 4% -> 5% of each run, Pallas kernels for 0% -> 0%
where the time goes in v3:
time: 21.4 us; the launch traced here: 21.2 us
  starting transfers between devices  7.73 us (36%)
  blocking collectives  6.26 us (29%)
  Pallas kernels  4.29 us (20%)
  local copies, waits for them, and re-layouts  1.69 us (8%)
  waiting for transfers between devices  1.11 us (5%)
    all_gather x1, blocking collectives, local(): blocks = lax.all_gather(packed, 'func', axis=0, tiled=False)  6.26 us
    ppermute x2, starting transfers between devices, swap_far(): return lax.ppermute(cells, 'tile', pairs)  4.79 us
    pallas_call x1, Pallas kernels, local(): pl.pallas_call(kernel, out_shape=jax.ShapeDtypeStruct(seeds.shape, jnp.fl...  4.29 us
    ppermute x2, starting transfers between devices, swap_near(): return lax.ppermute(cells, 'tile', [(i, i ^ 1) for i in range(count)])  2.94 us
    ppermute x2, waiting for transfers between devices, swap_far(): return lax.ppermute(cells, 'tile', pairs)  1.11 us
    dynamic_slice x1, local copies, waits for them, and re-layouts, local(): lax.dynamic_slice_in_dim(seeds, jnp.where(even, 0, tail), RIM, axis=2)  0.98 us
    unnamed x4, local copies, waits for them, and re-layouts  0.7 us
  transfers between devices with their start and end apart: 4, of which 1 were waited for; matrix products, arithmetic and copies ran while one was open for 5% of the time, Pallas kernels for 0%

profile of v3, /device:TPU:0, one launch (start us, length us, event | category | flops | bytes accessed | tf_op | source)
XLA Modules:
  0.0 21.2 jit_solution(7678854495169117095)
XLA Ops:
  0.0 2.9 %collective-permute-start.3 = (f32[2,5,8,128]{3,2,1,0:T(8,128)}, f32[2,5,8,128]{3,2,1,0:T(8,128)S(1)}, u32[]{:S(2)}, u32[]{:S(2)}) collective-permute-start(f32[2,5,8,128]{3,2,1,0:T(8,128)} %param.3), channel_id=1, source_target_pairs={{0,4},{4,0},{8,12},{12,8},{16,20},{20,16},{24,28},{28,24},{1,5},{5... | collective-permute-start | bytes 122888 | tf_op jit(solution)/shard_map/ppermute | solution.py:28
  2.9 3.6 %collective-permute-start.2 = (f32[2,5,8,128]{3,2,1,0:T(8,128)}, f32[2,5,8,128]{3,2,1,0:T(8,128)S(1)}, u32[]{:S(2)}, u32[]{:S(2)}) collective-permute-start(f32[2,5,8,128]{3,2,1,0:T(8,128)} %param.3), channel_id=1, source_target_pairs={{0,28},{4,8},{8,4},{12,16},{16,12},{20,24},{24,20},{28,0},{1,29},{... | collective-permute-start | bytes 122888 | tf_op jit(solution)/shard_map/ppermute | solution.py:34
  6.5 1.0 %constant_dynamic-slice_fusion = (f32[3,5,16,128]{3,2,1,0:T(8,128)S(1)}, f32[3,5,16,128]{3,2,1,0:T(8,128)S(1)}) fusion(f32[3,5,32,128]{3,2,1,0:T(8,128)} %seeds_ref.1, s32[]{:T(128)S(6)} %select_n.29, s32[]{:T(128)S(6)} %select_n.28), kind=kLoop, calls=%fused_computation.8 | loop fusion | bytes 491528 | tf_op jit(solution)/shard_map/dynamic_slice | solution.py:257
  7.5 1.2 %collective-permute-start.1 = (f32[3,5,16,128]{3,2,1,0:T(8,128)S(1)}, f32[3,5,16,128]{3,2,1,0:T(8,128)S(1)}, u32[]{:S(2)}, u32[]{:S(2)}) collective-permute-start(f32[3,5,16,128]{3,2,1,0:T(8,128)S(1)} %get-tuple-element.5), channel_id=1, source_target_pairs={{0,28},{4,8},{8,4},{12,16},{16,12},{20,24},{24,20},{28,0},{1,29},{... | collective-permute-start | bytes 368648 | tf_op jit(solution)/shard_map/ppermute | solution.py:34
  8.7 0.0 collective-permute-start
  8.7 0.0 collective-permute-done.3
  8.7 1.1 %collective-permute-done.2 = f32[2,5,8,128]{3,2,1,0:T(8,128)S(1)} collective-permute-done((f32[2,5,8,128]{3,2,1,0:T(8,128)}, f32[2,5,8,128]{3,2,1,0:T(8,128)S(1)}, u32[]{:S(2)}, u32[]{:S(2)}) %collective-permute-start.2) | collective-permute-done | bytes 40992 | tf_op jit(solution)/shard_map/ppermute | solution.py:34
  9.9 0.0 copy-start.1
  9.9 0.1 fusion
  9.9 0.7 %copy-done.1 = f32[2,5,8,128]{3,2,1,0:T(8,128)S(1)} copy-done((f32[2,5,8,128]{3,2,1,0:T(8,128)S(1)}, f32[2,5,8,128]{3,2,1,0:T(8,128)}, u32[]{:S(2)}) %copy-start.1) | copy-done | bytes 40984
  10.7 0.0 copy-start
  10.7 6.3 %all-gather = f32[80,8,128]{2,1,0:T(8,128)S(1)} all-gather(f32[20,8,128]{2,1,0:T(8,128)S(1)} %pad_maximum_fusion), channel_id=2, replica_groups=mesh['tile'=8,'func'=4] {'func'}, dimensions={0}, use_global_device_ids=true | all-gather | bytes 409600 | tf_op jit(solution)/shard_map/all_gather | solution.py:269
  16.9 0.0 collective-permute-done.1.far_ref
  16.9 0.0 collective-permute-done.near_ref
  16.9 0.0 copy-done
  16.9 4.3 %two_steps.1 = f32[3,5,32,128]{3,2,1,0:T(8,128)} custom-call(f32[3,5,32,128]{3,2,1,0:T(8,128)S(1)} %copy-done, f32[3,5,16,128]{3,2,1,0:T(8,128)S(1)} %collective-permute-done.near_ref, f32[3,5,16,128]{3,2,1,0:T(8,128)S(1)} %collective-permute-done.1.far_ref, f32[4,20,8,128]{3,2,1,0:T(8,128)S(1)} %bitcast.12), custom_call_target="tpu_custom_call" | custom-call | tf_op jit(solution)/shard_map/two_steps/pallas_call | solution.py:285
  (4 shorter events, 0.0 us)
Async XLA Ops:
  0.0 8.7 %collective-permute-start.3 = (f32[2,5,8,128]{3,2,1,0:T(8,128)}, f32[2,5,8,128]{3,2,1,0:T(8,128)S(1)}, u32[]{:S(2)}, u32[]{:S(2)}) collective-permute-start(f32[2,5,8,128]{3,2,1,0:T(8,128)} %param.3), channel_id=1, source_target_pairs={{0,4},{4,0},{8,12},{12,8},{16,20},{20,16},{24,28},{28,24},{1,5},{5... | collective-permute-start | bytes 122888 | tf_op jit(solution)/shard_map/ppermute | solution.py:28
  2.9 6.9 %collective-permute-start.2 = (f32[2,5,8,128]{3,2,1,0:T(8,128)}, f32[2,5,8,128]{3,2,1,0:T(8,128)S(1)}, u32[]{:S(2)}, u32[]{:S(2)}) collective-permute-start(f32[2,5,8,128]{3,2,1,0:T(8,128)} %param.3), channel_id=1, source_target_pairs={{0,28},{4,8},{8,4},{12,16},{16,12},{20,24},{24,20},{28,0},{1,29},{... | collective-permute-start | bytes 122888 | tf_op jit(solution)/shard_map/ppermute | solution.py:34
  7.5 9.4 %collective-permute-start.1 = (f32[3,5,16,128]{3,2,1,0:T(8,128)S(1)}, f32[3,5,16,128]{3,2,1,0:T(8,128)S(1)}, u32[]{:S(2)}, u32[]{:S(2)}) collective-permute-start(f32[3,5,16,128]{3,2,1,0:T(8,128)S(1)} %get-tuple-element.5), channel_id=1, source_target_pairs={{0,28},{4,8},{8,4},{12,16},{16,12},{20,24},{24,20},{28,0},{1,29},{... | collective-permute-start | bytes 368648 | tf_op jit(solution)/shard_map/ppermute | solution.py:34
  8.7 8.2 %collective-permute-start = (f32[3,5,16,128]{3,2,1,0:T(8,128)S(1)}, f32[3,5,16,128]{3,2,1,0:T(8,128)S(1)}, u32[]{:S(2)}, u32[]{:S(2)}) collective-permute-start(f32[3,5,16,128]{3,2,1,0:T(8,128)S(1)} %get-tuple-element.6), channel_id=1, source_target_pairs={{0,4},{4,0},{8,12},{12,8},{16,20},{20,16},{24,28},{28,24},{1,5},{5... | collective-permute-start | bytes 368648 | tf_op jit(solution)/shard_map/ppermute | solution.py:28
  9.9 0.8 %copy-start.1 = (f32[2,5,8,128]{3,2,1,0:T(8,128)S(1)}, f32[2,5,8,128]{3,2,1,0:T(8,128)}, u32[]{:S(2)}) copy-start(f32[2,5,8,128]{3,2,1,0:T(8,128)} %param.3) | copy-start | bytes 122884
  10.7 6.3 %copy-start = (f32[3,5,32,128]{3,2,1,0:T(8,128)S(1)}, f32[3,5,32,128]{3,2,1,0:T(8,128)}, u32[]{:S(2)}) copy-start(f32[3,5,32,128]{3,2,1,0:T(8,128)} %seeds_ref.1) | copy-start | bytes 737284

commit v4 on v3

v4 whole, which is shorter than its diff:
```python
from itertools import chain

import jax
import jax.numpy as jnp
from jax import lax
from jax.experimental import pallas as pl
from jax.experimental.pallas import tpu as pltpu
from jax.sharding import PartitionSpec as P

NZ = 4
STEPS = 2
FIELDS = 5
LANES = 128
SUB = 8

step_size = 0.3
twelfth = step_size / 12.0

RIM = 16
BASE_RIM = 24
LONG_RIM = 20
SHORT_RIM = 12
STATE_RIMS = (SHORT_RIM, LONG_RIM)
START_EVERY, STORES = 2, 2
STILL = (1.0, 0.0, 0.0, 0.0, 2.5)
STATE_EDGES = ((8, 8, 16, 16), (0, 0, 8, 8))


def swap_near(cells):
    count = lax.axis_size("tile")
    return lax.ppermute(cells, "tile", [(i, i ^ 1) for i in range(count)])


def swap_far(cells):
    count = lax.axis_size("tile")
    pairs = [(i, (i + (1 if i % 2 else -1)) % count) for i in range(count)]
    return lax.ppermute(cells, "tile", pairs)


def second_weights():
    shape = (LANES, LANES)
    ahead = lax.broadcasted_iota(jnp.int32, shape, 0) - lax.broadcasted_iota(jnp.int32, shape, 1)
    ahead = jnp.bitwise_and(ahead, LANES - 1)
    weights = jnp.zeros(shape, jnp.float32)
    for places, weight in ((NZ, 8.0), (-NZ, -8.0), (2 * NZ, -1.0), (-2 * NZ, 1.0)):
        weights = jnp.where(ahead == places % LANES, weight, weights)
    return jnp.concatenate([weights, weights], axis=0).astype(jnp.bfloat16)


def first_weights(count, total, skip):
    shape = (count, 2 * total)
    column = lax.broadcasted_iota(jnp.int32, shape, 1)
    column = jnp.where(column < total, column, column - total)
    ahead = column - lax.broadcasted_iota(jnp.int32, shape, 0) - skip
    weights = jnp.zeros(shape, jnp.float32)
    for places, weight in ((1, 8.0), (-1, -8.0), (2, -1.0), (-2, 1.0)):
        weights = jnp.where(ahead == places, weight, weights)
    return weights.astype(jnp.bfloat16)


def parts(cells):
    high = cells.astype(jnp.bfloat16)
    return high, (cells - high.astype(jnp.float32)).astype(jnp.bfloat16)


def second_diff(high, low, weights):
    fields, count, _ = high.shape
    cells = jnp.concatenate([high, low], axis=2).reshape(fields * count, 2 * LANES)
    return jnp.dot(cells, weights, preferred_element_type=jnp.float32)


def first_diff(high, low, weights):
    cells = jnp.concatenate([high, low], axis=1)
    cells = jnp.concatenate([cells[k] for k in range(FIELDS)], axis=1)
    return jnp.dot(weights, cells, preferred_element_type=jnp.float32)


def lanes(k):
    return slice(k * LANES, (k + 1) * LANES)


def primitives(state):
    density, mom_x, mom_y, mom_z, energy = state
    inverse = 1.0 / density
    vel_x, vel_y, vel_z = mom_x * inverse, mom_y * inverse, mom_z * inverse
    half = 0.5 * (vel_x * vel_x + vel_y * vel_y + vel_z * vel_z)
    press = 0.4 * (energy - density * half)
    total = energy + press
    return vel_x, vel_y, vel_z, total * inverse, half, press, total


def together(works):
    done = object()
    while works:
        works = [work for work in works if next(work, done) is not done]


def tiles(start, stop):
    return [slice(place, place + SUB) for place in range(start, stop, SUB)]


def within(cells, rows, edge, span, k):
    if edge <= rows.start and rows.stop <= span - edge:
        return cells
    place = rows.start + lax.broadcasted_iota(jnp.int32, cells.shape, 0)
    return jnp.where(jnp.logical_and(place >= edge, place < span - edge), cells, STILL[k])


def state_stage(stage, moment, base_ref, coef_ref, now_ref, flux_ref, slope_ref, lefts, weights, span):
    here, there = STATE_EDGES[moment][stage], STATE_EDGES[moment][min(stage + 1, 3)]
    for rows in tiles(here, span - here):
        source_ref = base_ref if stage == 0 else now_ref
        state = [source_ref[moment, k, rows] for k in range(FIELDS)]
        vel_x, vel_y, vel_z, heat, half, press, total = primitives(state)
        for k, cells in enumerate((vel_x, vel_y, vel_z, heat, half)):
            coef_ref[moment, stage, k, rows] = cells
        if stage == 3:
            continue
        _, mom_x, mom_y, mom_z, _ = state
        cross = mom_x * vel_y
        first = (mom_x, mom_x * vel_x + press, cross, mom_z * vel_x, total * vel_x)
        second = (mom_y, cross, mom_y * vel_y + press, mom_z * vel_y, total * vel_y)
        for k in range(FIELDS):
            flux_ref[moment, k, rows] = first[k]
            if there <= rows.start < span - there:
                slope_ref[moment, k, rows] = second[k]
    if stage == 3:
        return
    count, total_rows = span - 2 * there, span - 2 * here
    left = lefts[count, total_rows]
    flux = flux_ref[moment, :, here : span - here]
    first = first_diff(*parts(flux), left)
    slope = slope_ref[moment, :, there : span - there]
    second = second_diff(*parts(slope), weights)
    second = second.reshape(FIELDS, count, LANES)
    yield
    scale = (0.5 if stage < 2 else 1.0) * twelfth
    for k in range(FIELDS):
        for rows in tiles(there, span - there):
            local_rows = slice(rows.start - there, rows.stop - there)
            slope = first[local_rows, lanes(k)] + second[k, local_rows]
            cells = base_ref[moment, k, rows] - scale * slope
            now_ref[moment, k, rows] = within(cells, rows, BASE_RIM - STATE_RIMS[moment] + 2 * (stage + 1), span, k)


def pull_differences(moment, stage, one, adj_ref, hold_ref, first_ref, second_ref, lefts, weights):
    tall = adj_ref.shape[2]
    start = (STEPS - 1 - moment) * SUB
    edge = start + SUB if stage == 0 else start
    source_ref = adj_ref if stage == 3 else hold_ref.at[2 - stage]
    total = tall - 2 * start
    high, low = parts(source_ref[one, :, start : tall - start])
    second = second_diff(high, low, weights).reshape(FIELDS, total, LANES)
    yield True
    first = first_diff(high, low, lefts[tall - 2 * edge, total])
    yield False
    for k in range(FIELDS):
        second_ref[one, k, start : tall - start] = second[k]
        yield True
        first_ref[one, edge : tall - edge, lanes(k)] = first[:, lanes(k)]
        yield True


def pull_stage(moment, stage, one, coef_ref, adj_ref, hold_ref, first_ref, second_ref, out_ref):
    tall = adj_ref.shape[2]
    shift, last = BASE_RIM - RIM, moment == 0
    start = (STEPS - 1 - moment) * SUB
    edge = start + SUB if stage == 0 else start
    for rows in tiles(edge, tall - edge):
        base_rows = slice(rows.start + shift, rows.stop + shift)
        vel_x, vel_y, vel_z, heat, half = [coef_ref[moment, stage, k, base_rows] for k in range(5)]
        a = [first_ref[one, rows, lanes(k)] for k in range(FIELDS)]
        b = [second_ref[one, k, rows] for k in range(FIELDS)]
        mix_x = vel_x * a[1] + vel_y * a[2] + vel_z * a[3] + heat * a[4]
        mix_y = vel_x * b[1] + vel_y * b[2] + vel_z * b[3] + heat * b[4]
        lift = vel_x * a[4] + vel_y * b[4]
        press = 0.4 * (a[1] + b[2] + lift)
        term = (
            half * press - vel_x * mix_x - vel_y * mix_y,
            a[0] + mix_x + vel_x * (a[1] - press) + vel_y * b[1],
            b[0] + mix_y + vel_y * (b[2] - press) + vel_x * a[2],
            vel_x * a[3] + vel_y * b[3] - vel_z * press,
            lift + press,
        )
        for k in range(FIELDS):
            adj = adj_ref[one, k, rows]
            if stage > 0:
                scale = (1.0 if stage == 1 else 0.5) * twelfth
                hold_ref[3 - stage, one, k, rows] = adj + scale * term[k]
                continue
            one_third, two_thirds, rest = [hold_ref[place, one, k, rows] for place in range(3)]
            mean = (one_third - adj + rest + 2.0 * two_thirds) * (1.0 / 3.0)
            result = mean + (twelfth / 6.0) * term[k]
            if last:
                out_ref[one, k, rows.start - RIM : rows.stop - RIM] = result
            else:
                adj_ref[one, k, rows] = result
        yield


def kernel(
    seeds_ref, near_ref, far_ref, blocks_ref, out_ref,
    adj_ref, hold_ref, first_ref, second_ref,
    base_ref, coef_ref, now_ref, flux_ref, slope_ref,
):
    funcs, _, strip, _ = seeds_ref.shape
    spread, _, block, _ = blocks_ref.shape
    tall, span = strip + 2 * RIM, strip + 2 * BASE_RIM
    even = lax.rem(lax.axis_index("tile"), 2) == 0

    def lay(left_ref, right_ref):
        for one in range(funcs):
            for k in range(FIELDS):
                adj_ref[one, k, :RIM] = left_ref[one, k]
                adj_ref[one, k, RIM + strip :] = right_ref[one, k]

    def lay_base(part, moment, shift, low, high):
        for owner in range(spread):
            start, stop = max(low, owner * block), min(high, (owner + 1) * block)
            if start < stop:
                rows = slice(start - owner * block, stop - owner * block)
                place = BASE_RIM + shift + start
                for k in range(FIELDS):
                    base_ref[moment, k, place : place + stop - start, :] = blocks_ref[owner, part * FIELDS + k, rows, :]

    for moment in range(STEPS):
        edge = BASE_RIM - STATE_RIMS[moment]
        for start in (STATE_EDGES[moment][0], span - STATE_EDGES[moment][0] - SUB):
            if start < edge or start + SUB > span - edge:
                for k in range(FIELDS):
                    base_ref[moment, k, start : start + SUB] = jnp.full((SUB, LANES), STILL[k], jnp.float32)
    middle = strip // 2
    lay_base(0, 0, 0, 0, strip)
    lay_base(1, 1, 0, 0, strip)
    lay_base(2, 1, strip, 0, middle)
    lay_base(2, 1, -strip, middle, strip)
    lay_base(3, 0, strip, 0, SHORT_RIM)
    lay_base(3, 1, -strip, max(SHORT_RIM, strip - LONG_RIM), middle)
    lay_base(3, 1, strip, middle, min(LONG_RIM, strip - SHORT_RIM))
    lay_base(3, 0, -strip, strip - SHORT_RIM, strip)

    weights = second_weights()
    sizes = {(tall - 2 * start, tall - 2 * start) for start in range(0, STEPS * SUB, SUB)}
    sizes |= {(tall - 2 * start - 2 * SUB, tall - 2 * start) for start in range(0, STEPS * SUB, SUB)}
    for edges in STATE_EDGES:
        sizes |= {(span - 2 * edges[n + 1], span - 2 * edges[n]) for n in range(3)}
    lefts = {size: first_weights(*size, (size[1] - size[0]) // 2) for size in sorted(sizes)}
    def states(moment):
        for stage in range(4):
            yield from state_stage(
                stage, moment, base_ref, coef_ref, now_ref, flux_ref, slope_ref, lefts, weights, span
            )

    def differences(moment, stage, one):
        return pull_differences(moment, stage, one, adj_ref, hold_ref, first_ref, second_ref, lefts, weights)

    pl.when(even)(lambda: lay(far_ref, near_ref))
    pl.when(jnp.logical_not(even))(lambda: lay(near_ref, far_ref))
    for one in range(funcs):
        for k in range(FIELDS):
            adj_ref[one, k, RIM : RIM + strip] = seeds_ref[one, k]
    together([chain(*(differences(STEPS - 1, 3, one) for one in range(funcs))), states(1), states(0)])
    starting, storing = iter(()), iter(())
    for moment in reversed(range(STEPS)):
        for stage in (3, 2, 1, 0):
            for one in range(funcs):
                work = pull_stage(moment, stage, one, coef_ref, adj_ref, hold_ref, first_ref, second_ref, out_ref)
                begun = False
                for number, _ in enumerate(work):
                    if number % START_EVERY == 0 and not begun:
                        begun = next(starting, False) is False
                    for _ in range(STORES):
                        next(storing, None)
                while not begun:
                    begun = next(starting, False) is False
                for _ in storing:
                    pass
                storing, starting = starting, iter(())
                if stage > 0:
                    starting = differences(moment, stage - 1, one)
                elif moment > 0:
                    starting = differences(moment - 1, 3, one)


def local(seeds, checkpoints):
    funcs, _, strip, _ = seeds.shape
    block = checkpoints.shape[2]
    even = lax.rem(lax.axis_index("tile"), 2) == 0
    far_base, near_base = swap_far(checkpoints), swap_near(checkpoints)
    tail = strip - RIM
    far_edge = lax.dynamic_slice_in_dim(seeds, jnp.where(even, 0, tail), RIM, axis=2)
    near_edge = lax.dynamic_slice_in_dim(seeds, jnp.where(even, tail, 0), RIM, axis=2)
    own = checkpoints.reshape(STEPS * FIELDS, block, LANES)
    roomy = jnp.pad(own, ((0, STEPS * FIELDS), (0, 0), (0, 0)))
    roomy, far_edge, near_edge = lax.optimization_barrier((roomy, far_edge, near_edge))
    far, near = swap_far(far_edge), swap_near(near_edge)
    lower = lax.axis_index("func") * block < strip // 2
    take_far = even != lower
    main = lax.select(take_far, far_base, near_base)
    other = lax.select(take_far, near_base[1], far_base[1])
    place = lax.axis_index("func") * block + lax.broadcasted_iota(jnp.int32, (1, block, 1), 1)
    inner = jnp.logical_and(place >= SHORT_RIM, place < strip - SHORT_RIM)
    rest = jnp.where(inner, other, main[0])
    packed = lax.dynamic_update_slice(roomy, jnp.concatenate([main[1], rest], axis=0), (STEPS * FIELDS, 0, 0))
    blocks = lax.all_gather(packed, "func", axis=0, tiled=False)
    tall, span = strip + 2 * RIM, strip + 2 * BASE_RIM
    shapes = [
        (funcs, FIELDS, tall, LANES),
        (3, funcs, FIELDS, tall, LANES),
        (funcs, tall, FIELDS * LANES),
        (funcs, FIELDS, tall, LANES),
        (STEPS, FIELDS, span, LANES),
        (STEPS, 4, 5, span, LANES),
        (STEPS, FIELDS, span, LANES),
        (STEPS, FIELDS, span, LANES),
        (STEPS, FIELDS, span, LANES),
    ]
    vmem = pl.BlockSpec(memory_space=pltpu.VMEM)
    return pl.pallas_call(
        kernel,
        out_shape=jax.ShapeDtypeStruct(seeds.shape, jnp.float32),
        in_specs=[vmem] * 4,
        out_specs=vmem,
        scratch_shapes=[pltpu.VMEM(shape, jnp.float32) for shape in shapes],
        compiler_params=pltpu.CompilerParams(vmem_limit_bytes=32 * 1024 * 1024),
        name="two_steps",
    )(seeds, near, far, blocks)


def solution(mesh):
    return jax.shard_map(
        local,
        mesh=mesh,
        in_specs=(P("func", None, "tile", None), P(None, None, ("tile", "func"), None)),
        out_specs=P("func", None, "tile", None),
        check_vma=False,
    )
```

time: 21.4 us -> 20.7 us (0.967)
  waiting for transfers between devices: 1.11 us -> 0.01 us
  starting transfers between devices: 7.73 us -> 8.48 us
  Pallas kernels: 4.29 us -> 3.77 us
    ppermute x2, waiting for transfers between devices: 1.11 us -> 0.01 us  [swap_far(): return lax.ppermute(cells, 'tile', pairs)]
    pad x0 -> x1, local copies, waits for them, and re-layouts: none -> 0.82 us  [local(): roomy = jnp.pad(own, ((0, STEPS * FIELDS), (0, 0), (0, 0)))]
    unnamed x4 -> x2, local copies, waits for them, and re-layouts: 0.7 us -> 0.01 us
    ppermute x2, starting transfers between devices: 4.79 us -> 5.47 us  [swap_far(): return lax.ppermute(cells, 'tile', pairs)]
    pallas_call x1, Pallas kernels: 4.29 us -> 3.77 us  [local(): pl.pallas_call(kernel, out_shape=jax.ShapeDtypeStruct(seeds.shape, jnp.fl...]
  transfers between devices with their start and end apart: 4 -> 4, of which waited for: 1 -> 0; matrix products, arithmetic and copies ran while one was open for 5% -> 9% of each run, Pallas kernels for 0% -> 0%
where the time goes in v4:
time: 20.7 us; the launch traced here: 20.5 us
  starting transfers between devices  8.48 us (41%)
  blocking collectives  6.26 us (30%)
  Pallas kernels  3.77 us (18%)
  local copies, waits for them, and re-layouts  1.8 us (9%)
    all_gather x1, blocking collectives, local(): blocks = lax.all_gather(packed, 'func', axis=0, tiled=False)  6.26 us
    ppermute x2, starting transfers between devices, swap_far(): return lax.ppermute(cells, 'tile', pairs)  5.47 us
    pallas_call x1, Pallas kernels, local(): pl.pallas_call(kernel, out_shape=jax.ShapeDtypeStruct(seeds.shape, jnp.fl...  3.77 us
    ppermute x2, starting transfers between devices, swap_near(): return lax.ppermute(cells, 'tile', [(i, i ^ 1) for i in range(count)])  3.01 us
    dynamic_slice x1, local copies, waits for them, and re-layouts, local(): lax.dynamic_slice_in_dim(seeds, jnp.where(even, tail, 0), RIM, axis=2)  0.98 us
    pad x1, local copies, waits for them, and re-layouts, local(): roomy = jnp.pad(own, ((0, STEPS * FIELDS), (0, 0), (0, 0)))  0.82 us
  transfers between devices with their start and end apart: 4, of which 0 were waited for; matrix products, arithmetic and copies ran while one was open for 9% of the time, Pallas kernels for 0%

profile of v4, /device:TPU:0, one launch (start us, length us, event | category | flops | bytes accessed | tf_op | source)
XLA Modules:
  0.0 20.5 jit_solution(17174092136790084157)
XLA Ops:
  0.0 2.9 %collective-permute-start.3 = (f32[2,5,8,128]{3,2,1,0:T(8,128)}, f32[2,5,8,128]{3,2,1,0:T(8,128)S(1)}, u32[]{:S(2)}, u32[]{:S(2)}) collective-permute-start(f32[2,5,8,128]{3,2,1,0:T(8,128)} %param.3), channel_id=1, source_target_pairs={{0,4},{4,0},{8,12},{12,8},{16,20},{20,16},{24,28},{28,24},{1,5},{5... | collective-permute-start | bytes 122888 | tf_op jit(solution)/shard_map/ppermute | solution.py:31
  2.9 3.6 %collective-permute-start.2 = (f32[2,5,8,128]{3,2,1,0:T(8,128)}, f32[2,5,8,128]{3,2,1,0:T(8,128)S(1)}, u32[]{:S(2)}, u32[]{:S(2)}) collective-permute-start(f32[2,5,8,128]{3,2,1,0:T(8,128)} %param.3), channel_id=1, source_target_pairs={{0,28},{4,8},{8,4},{12,16},{16,12},{20,24},{24,20},{28,0},{1,29},{... | collective-permute-start | bytes 122888 | tf_op jit(solution)/shard_map/ppermute | solution.py:37
  6.5 0.8 %pad.4 = f32[20,8,128]{2,1,0:T(8,128)S(1)} pad(f32[10,8,128]{2,1,0:T(8,128)} %bitcast.17, f32[]{:T(128)} %constant.9.clone.1), padding=0_10x0_0x0_0 | pad | bytes 122884 | tf_op jit(solution)/shard_map/jit(_pad)/pad | solution.py:294
  7.3 1.0 %constant_dynamic-slice_fusion = (f32[3,5,16,128]{3,2,1,0:T(8,128)S(1)}, f32[3,5,16,128]{3,2,1,0:T(8,128)S(1)}) fusion(f32[3,5,32,128]{3,2,1,0:T(8,128)} %seeds_ref.1, s32[]{:T(128)S(6)} %select_n.29, s32[]{:T(128)S(6)} %select_n.28), kind=kLoop, calls=%fused_computation.9 | loop fusion | bytes 491528 | tf_op jit(solution)/shard_map/dynamic_slice | solution.py:292
  8.3 0.1 collective-permute-start
  8.4 1.9 %collective-permute-start.1 = (f32[3,5,16,128]{3,2,1,0:T(8,128)S(1)}, f32[3,5,16,128]{3,2,1,0:T(8,128)S(1)}, u32[]{:S(2)}, u32[]{:S(2)}) collective-permute-start(f32[3,5,16,128]{3,2,1,0:T(8,128)S(1)} %get-tuple-element.9), channel_id=1, source_target_pairs={{0,28},{4,8},{8,4},{12,16},{16,12},{20,24},{24,20},{28,0},{1,29},{... | collective-permute-start | bytes 368648 | tf_op jit(solution)/shard_map/ppermute | solution.py:37
  10.3 0.0 collective-permute-done.3
  10.3 0.0 collective-permute-done.2
  10.3 0.1 fusion.1
  10.4 0.0 copy-start
  10.4 6.3 %all_gather.10.blocks_ref = f32[4,20,8,128]{3,2,1,0:T(8,128)S(1)} all-gather(f32[1,20,8,128]{3,2,1,0:T(8,128)S(1)} %fusion), channel_id=1, replica_groups=mesh['tile'=8,'func'=4] {'func'}, dimensions={0}, use_global_device_ids=true | all-gather | bytes 409600 | tf_op jit(solution)/shard_map/all_gather | solution.py:305
  16.7 0.0 collective-permute-done.near_ref
  16.7 0.0 collective-permute-done.1.far_ref
  16.7 0.0 copy-done
  16.7 3.8 %two_steps.1 = f32[3,5,32,128]{3,2,1,0:T(8,128)} custom-call(f32[3,5,32,128]{3,2,1,0:T(8,128)S(1)} %copy-done, f32[3,5,16,128]{3,2,1,0:T(8,128)S(1)} %collective-permute-done.near_ref, f32[3,5,16,128]{3,2,1,0:T(8,128)S(1)} %collective-permute-done.1.far_ref, f32[4,20,8,128]{3,2,1,0:T(8,128)S(1)} %all_gather.10.blocks_ref), custom_call_target="tpu_custom_call" | custom-call | tf_op jit(solution)/shard_map/two_steps/pallas_call | solution.py:319
  (4 shorter events, 0.0 us)
Async XLA Ops:
  0.0 10.3 %collective-permute-start.3 = (f32[2,5,8,128]{3,2,1,0:T(8,128)}, f32[2,5,8,128]{3,2,1,0:T(8,128)S(1)}, u32[]{:S(2)}, u32[]{:S(2)}) collective-permute-start(f32[2,5,8,128]{3,2,1,0:T(8,128)} %param.3), channel_id=1, source_target_pairs={{0,4},{4,0},{8,12},{12,8},{16,20},{20,16},{24,28},{28,24},{1,5},{5... | collective-permute-start | bytes 122888 | tf_op jit(solution)/shard_map/ppermute | solution.py:31
  2.9 7.4 %collective-permute-start.2 = (f32[2,5,8,128]{3,2,1,0:T(8,128)}, f32[2,5,8,128]{3,2,1,0:T(8,128)S(1)}, u32[]{:S(2)}, u32[]{:S(2)}) collective-permute-start(f32[2,5,8,128]{3,2,1,0:T(8,128)} %param.3), channel_id=1, source_target_pairs={{0,28},{4,8},{8,4},{12,16},{16,12},{20,24},{24,20},{28,0},{1,29},{... | collective-permute-start | bytes 122888 | tf_op jit(solution)/shard_map/ppermute | solution.py:37
  8.3 8.4 %collective-permute-start = (f32[3,5,16,128]{3,2,1,0:T(8,128)S(1)}, f32[3,5,16,128]{3,2,1,0:T(8,128)S(1)}, u32[]{:S(2)}, u32[]{:S(2)}) collective-permute-start(f32[3,5,16,128]{3,2,1,0:T(8,128)S(1)} %get-tuple-element.8), channel_id=1, source_target_pairs={{0,4},{4,0},{8,12},{12,8},{16,20},{20,16},{24,28},{28,24},{1,5},{5... | collective-permute-start | bytes 368648 | tf_op jit(solution)/shard_map/ppermute | solution.py:31
  8.4 8.3 %collective-permute-start.1 = (f32[3,5,16,128]{3,2,1,0:T(8,128)S(1)}, f32[3,5,16,128]{3,2,1,0:T(8,128)S(1)}, u32[]{:S(2)}, u32[]{:S(2)}) collective-permute-start(f32[3,5,16,128]{3,2,1,0:T(8,128)S(1)} %get-tuple-element.9), channel_id=1, source_target_pairs={{0,28},{4,8},{8,4},{12,16},{16,12},{20,24},{24,20},{28,0},{1,29},{... | collective-permute-start | bytes 368648 | tf_op jit(solution)/shard_map/ppermute | solution.py:37
  10.4 6.3 %copy-start = (f32[3,5,32,128]{3,2,1,0:T(8,128)S(1)}, f32[3,5,32,128]{3,2,1,0:T(8,128)}, u32[]{:S(2)}) copy-start(f32[3,5,32,128]{3,2,1,0:T(8,128)} %seeds_ref.1) | copy-start | bytes 737284

commit v5 on v4

--- a/solution.py
+++ b/solution.py
@@ -199,7 +199,7 @@
 
 
 def kernel(
-    seeds_ref, near_ref, far_ref, blocks_ref, out_ref,
+    seeds_ref, far_ref, near_ref, blocks_ref, out_ref,
     adj_ref, hold_ref, first_ref, second_ref,
     base_ref, coef_ref, now_ref, flux_ref, slope_ref,
 ):
@@ -292,7 +292,7 @@
     near_edge = lax.dynamic_slice_in_dim(seeds, jnp.where(even, tail, 0), RIM, axis=2)
     own = checkpoints.reshape(STEPS * FIELDS, block, LANES)
     roomy = jnp.pad(own, ((0, STEPS * FIELDS), (0, 0), (0, 0)))
-    roomy, far_edge, near_edge = lax.optimization_barrier((roomy, far_edge, near_edge))
+    roomy, far_base = lax.optimization_barrier((roomy, far_base))
     far, near = swap_far(far_edge), swap_near(near_edge)
     lower = lax.axis_index("func") * block < strip // 2
     take_far = even != lower
@@ -324,7 +324,7 @@
         scratch_shapes=[pltpu.VMEM(shape, jnp.float32) for shape in shapes],
         compiler_params=pltpu.CompilerParams(vmem_limit_bytes=32 * 1024 * 1024),
         name="two_steps",
-    )(seeds, near, far, blocks)
+    )(seeds, far, near, blocks)
 
 
 def solution(mesh):

time: 20.7 us -> 20.2 us (0.976)
  local copies, waits for them, and re-layouts: 1.8 us -> 1.01 us
  waiting for transfers between devices: 0.01 us -> 0.39 us
    pad x1, local copies, waits for them, and re-layouts: 0.82 us -> 0.01 us  [local(): roomy = jnp.pad(own, ((0, STEPS * FIELDS), (0, 0), (0, 0)))]
    ppermute x2, waiting for transfers between devices: 0.01 us -> 0.39 us  [swap_far(): return lax.ppermute(cells, 'tile', pairs)]
  transfers between devices with their start and end apart: 4 -> 4, of which waited for: 0 -> 1; matrix products, arithmetic and copies ran while one was open for 9% -> 5% of each run, Pallas kernels for 0% -> 0%
where the time goes in v5:
time: 20.2 us; the launch traced here: 20 us
  starting transfers between devices  8.48 us (42%)
  blocking collectives  6.26 us (31%)
  Pallas kernels  3.75 us (19%)
  local copies, waits for them, and re-layouts  1.01 us (5%)
  waiting for transfers between devices  0.39 us (2%)
    all_gather x1, blocking collectives, local(): blocks = lax.all_gather(packed, 'func', axis=0, tiled=False)  6.26 us
    ppermute x2, starting transfers between devices, swap_far(): return lax.ppermute(cells, 'tile', pairs)  5.47 us
    pallas_call x1, Pallas kernels, local(): pl.pallas_call(kernel, out_shape=jax.ShapeDtypeStruct(seeds.shape, jnp.fl...  3.75 us
    ppermute x2, starting transfers between devices, swap_near(): return lax.ppermute(cells, 'tile', [(i, i ^ 1) for i in range(count)])  3.01 us
    dynamic_slice x1, local copies, waits for them, and re-layouts, local(): lax.dynamic_slice_in_dim(seeds, jnp.where(even, tail, 0), RIM, axis=2)  0.99 us
  transfers between devices with their start and end apart: 4, of which 1 were waited for; matrix products, arithmetic and copies ran while one was open for 5% of the time, Pallas kernels for 0%

profile of v5, /device:TPU:0, one launch (start us, length us, event | category | flops | bytes accessed | tf_op | source)
XLA Modules:
  0.0 20.0 jit_solution(6843885972460967955)
XLA Ops:
  0.0 2.9 %collective-permute-start.3 = (f32[2,5,8,128]{3,2,1,0:T(8,128)}, f32[2,5,8,128]{3,2,1,0:T(8,128)S(1)}, u32[]{:S(2)}, u32[]{:S(2)}) collective-permute-start(f32[2,5,8,128]{3,2,1,0:T(8,128)} %param.3), channel_id=1, source_target_pairs={{0,4},{4,0},{8,12},{12,8},{16,20},{20,16},{24,28},{28,24},{1,5},{5... | collective-permute-start | bytes 122888 | tf_op jit(solution)/shard_map/ppermute | solution.py:31
  2.9 3.6 %collective-permute-start.2 = (f32[2,5,8,128]{3,2,1,0:T(8,128)}, f32[2,5,8,128]{3,2,1,0:T(8,128)S(1)}, u32[]{:S(2)}, u32[]{:S(2)}) collective-permute-start(f32[2,5,8,128]{3,2,1,0:T(8,128)} %param.3), channel_id=1, source_target_pairs={{0,28},{4,8},{8,4},{12,16},{16,12},{20,24},{24,20},{28,0},{1,29},{... | collective-permute-start | bytes 122888 | tf_op jit(solution)/shard_map/ppermute | solution.py:37
  6.5 0.0 copy-start.1
  6.5 1.0 %constant_dynamic-slice_fusion = (f32[3,5,16,128]{3,2,1,0:T(8,128)S(1)}, f32[3,5,16,128]{3,2,1,0:T(8,128)S(1)}) fusion(f32[3,5,32,128]{3,2,1,0:T(8,128)} %seeds_ref.1, s32[]{:T(128)S(6)} %select_n.29, s32[]{:T(128)S(6)} %select_n.28), kind=kLoop, calls=%fused_computation.9 | loop fusion | bytes 491528 | tf_op jit(solution)/shard_map/dynamic_slice | solution.py:292
  7.5 0.1 collective-permute-start.1
  7.6 1.9 %collective-permute-start = (f32[3,5,16,128]{3,2,1,0:T(8,128)S(1)}, f32[3,5,16,128]{3,2,1,0:T(8,128)S(1)}, u32[]{:S(2)}, u32[]{:S(2)}) collective-permute-start(f32[3,5,16,128]{3,2,1,0:T(8,128)S(1)} %get-tuple-element.10), channel_id=1, source_target_pairs={{0,28},{4,8},{8,4},{12,16},{16,12},{20,24},{24,20},{28,0},{1,29},{... | collective-permute-start | bytes 368648 | tf_op jit(solution)/shard_map/ppermute | solution.py:37
  9.5 0.0 copy-done.1
  9.5 0.4 %collective-permute-done.2 = f32[2,5,8,128]{3,2,1,0:T(8,128)S(1)} collective-permute-done((f32[2,5,8,128]{3,2,1,0:T(8,128)}, f32[2,5,8,128]{3,2,1,0:T(8,128)S(1)}, u32[]{:S(2)}, u32[]{:S(2)}) %collective-permute-start.2) | collective-permute-done | bytes 40992 | tf_op jit(solution)/shard_map/ppermute | solution.py:37
  9.9 0.0 collective-permute-done.3
  9.9 0.1 fusion.1
  10.0 0.0 copy-start
  10.0 6.3 %all_gather.10.blocks_ref = f32[4,20,8,128]{3,2,1,0:T(8,128)S(1)} all-gather(f32[1,20,8,128]{3,2,1,0:T(8,128)S(1)} %fusion), channel_id=1, replica_groups=mesh['tile'=8,'func'=4] {'func'}, dimensions={0}, use_global_device_ids=true | all-gather | bytes 409600 | tf_op jit(solution)/shard_map/all_gather | solution.py:305
  16.3 0.0 collective-permute-done.1.near_ref
  16.3 0.0 collective-permute-done.far_ref
  16.3 0.0 copy-done
  16.3 3.8 %two_steps.1 = f32[3,5,32,128]{3,2,1,0:T(8,128)} custom-call(f32[3,5,32,128]{3,2,1,0:T(8,128)S(1)} %copy-done, f32[3,5,16,128]{3,2,1,0:T(8,128)S(1)} %collective-permute-done.far_ref, f32[3,5,16,128]{3,2,1,0:T(8,128)S(1)} %collective-permute-done.1.near_ref, f32[4,20,8,128]{3,2,1,0:T(8,128)S(1)} %all_gather.10.blocks_ref), custom_call_target="tpu_custom_call" | custom-call | tf_op jit(solution)/shard_map/two_steps/pallas_call | solution.py:319
  (5 shorter events, 0.0 us)
Async XLA Ops:
  0.0 9.9 %collective-permute-start.3 = (f32[2,5,8,128]{3,2,1,0:T(8,128)}, f32[2,5,8,128]{3,2,1,0:T(8,128)S(1)}, u32[]{:S(2)}, u32[]{:S(2)}) collective-permute-start(f32[2,5,8,128]{3,2,1,0:T(8,128)} %param.3), channel_id=1, source_target_pairs={{0,4},{4,0},{8,12},{12,8},{16,20},{20,16},{24,28},{28,24},{1,5},{5... | collective-permute-start | bytes 122888 | tf_op jit(solution)/shard_map/ppermute | solution.py:31
  2.9 7.0 %collective-permute-start.2 = (f32[2,5,8,128]{3,2,1,0:T(8,128)}, f32[2,5,8,128]{3,2,1,0:T(8,128)S(1)}, u32[]{:S(2)}, u32[]{:S(2)}) collective-permute-start(f32[2,5,8,128]{3,2,1,0:T(8,128)} %param.3), channel_id=1, source_target_pairs={{0,28},{4,8},{8,4},{12,16},{16,12},{20,24},{24,20},{28,0},{1,29},{... | collective-permute-start | bytes 122888 | tf_op jit(solution)/shard_map/ppermute | solution.py:37
  6.5 3.0 %copy-start.1 = (f32[2,5,8,128]{3,2,1,0:T(8,128)S(1)}, f32[2,5,8,128]{3,2,1,0:T(8,128)}, u32[]{:S(2)}) copy-start(f32[2,5,8,128]{3,2,1,0:T(8,128)} %param.3) | copy-start | bytes 122884
  7.5 8.8 %collective-permute-start.1 = (f32[3,5,16,128]{3,2,1,0:T(8,128)S(1)}, f32[3,5,16,128]{3,2,1,0:T(8,128)S(1)}, u32[]{:S(2)}, u32[]{:S(2)}) collective-permute-start(f32[3,5,16,128]{3,2,1,0:T(8,128)S(1)} %get-tuple-element.9), channel_id=1, source_target_pairs={{0,4},{4,0},{8,12},{12,8},{16,20},{20,16},{24,28},{28,24},{1,5},{5... | collective-permute-start | bytes 368648 | tf_op jit(solution)/shard_map/ppermute | solution.py:31
  7.6 8.7 %collective-permute-start = (f32[3,5,16,128]{3,2,1,0:T(8,128)S(1)}, f32[3,5,16,128]{3,2,1,0:T(8,128)S(1)}, u32[]{:S(2)}, u32[]{:S(2)}) collective-permute-start(f32[3,5,16,128]{3,2,1,0:T(8,128)S(1)} %get-tuple-element.10), channel_id=1, source_target_pairs={{0,28},{4,8},{8,4},{12,16},{16,12},{20,24},{24,20},{28,0},{1,29},{... | collective-permute-start | bytes 368648 | tf_op jit(solution)/shard_map/ppermute | solution.py:37
  10.0 6.3 %copy-start = (f32[3,5,32,128]{3,2,1,0:T(8,128)S(1)}, f32[3,5,32,128]{3,2,1,0:T(8,128)}, u32[]{:S(2)}) copy-start(f32[3,5,32,128]{3,2,1,0:T(8,128)} %seeds_ref.1) | copy-start | bytes 737284

commit v6 on v4

--- a/solution.py
+++ b/solution.py
@@ -29,6 +29,11 @@
 def swap_near(cells):
     count = lax.axis_size("tile")
     return lax.ppermute(cells, "tile", [(i, i ^ 1) for i in range(count)])
+
+
+def shift(cells, places):
+    count = lax.axis_size("tile")
+    return lax.ppermute(cells, "tile", [(i, (i + places) % count) for i in range(count)])
 
 
 def swap_far(cells):
@@ -286,18 +291,17 @@
     funcs, _, strip, _ = seeds.shape
     block = checkpoints.shape[2]
     even = lax.rem(lax.axis_index("tile"), 2) == 0
-    far_base, near_base = swap_far(checkpoints), swap_near(checkpoints)
+    left, right = shift(checkpoints, 1), shift(checkpoints, -1)
     tail = strip - RIM
     far_edge = lax.dynamic_slice_in_dim(seeds, jnp.where(even, 0, tail), RIM, axis=2)
     near_edge = lax.dynamic_slice_in_dim(seeds, jnp.where(even, tail, 0), RIM, axis=2)
     own = checkpoints.reshape(STEPS * FIELDS, block, LANES)
     roomy = jnp.pad(own, ((0, STEPS * FIELDS), (0, 0), (0, 0)))
-    roomy, far_edge, near_edge = lax.optimization_barrier((roomy, far_edge, near_edge))
+    roomy, right = lax.optimization_barrier((roomy, right))
     far, near = swap_far(far_edge), swap_near(near_edge)
     lower = lax.axis_index("func") * block < strip // 2
-    take_far = even != lower
-    main = lax.select(take_far, far_base, near_base)
-    other = lax.select(take_far, near_base[1], far_base[1])
+    main = lax.select(lower, right, left)
+    other = lax.select(lower, left[1], right[1])
     place = lax.axis_index("func") * block + lax.broadcasted_iota(jnp.int32, (1, block, 1), 1)
     inner = jnp.logical_and(place >= SHORT_RIM, place < strip - SHORT_RIM)
     rest = jnp.where(inner, other, main[0])

time: 20.7 us -> 19.8 us (0.957)
  local copies, waits for them, and re-layouts: 1.8 us -> 1.01 us
  starting transfers between devices: 8.48 us -> 8.07 us
  waiting for transfers between devices: 0.01 us -> 0.42 us
    ppermute x0 -> x2, starting transfers between devices: none -> 5.98 us  [shift(): lax.ppermute(cells, 'tile', [(i, (i + places) % count) for i in range(cou...]
    ppermute x2 -> x1, starting transfers between devices: 5.47 us -> 2.09 us  [swap_far(): return lax.ppermute(cells, 'tile', pairs)]
    ppermute x2 -> x1, starting transfers between devices: 3.01 us -> 0.01 us  [swap_near(): return lax.ppermute(cells, 'tile', [(i, i ^ 1) for i in range(count)])]
    pad x1, local copies, waits for them, and re-layouts: 0.82 us -> 0.01 us  [local(): roomy = jnp.pad(own, ((0, STEPS * FIELDS), (0, 0), (0, 0)))]
    ppermute x2 -> x1, waiting for transfers between devices: 0.01 us -> 0.41 us  [swap_near(): return lax.ppermute(cells, 'tile', [(i, i ^ 1) for i in range(count)])]
  transfers between devices with their start and end apart: 4 -> 4, of which waited for: 0 -> 1; matrix products, arithmetic and copies ran while one was open for 9% -> 6% of each run, Pallas kernels for 0% -> 0%
where the time goes in v6:
time: 19.8 us; the launch traced here: 19.7 us
  starting transfers between devices  8.07 us (41%)
  blocking collectives  6.26 us (32%)
  Pallas kernels  3.76 us (19%)
  local copies, waits for them, and re-layouts  1.01 us (5%)
  waiting for transfers between devices  0.42 us (2%)
    all_gather x1, blocking collectives, local(): blocks = lax.all_gather(packed, 'func', axis=0, tiled=False)  6.26 us
    ppermute x2, starting transfers between devices, shift(): lax.ppermute(cells, 'tile', [(i, (i + places) % count) for i in range(cou...  5.98 us
    pallas_call x1, Pallas kernels, local(): pl.pallas_call(kernel, out_shape=jax.ShapeDtypeStruct(seeds.shape, jnp.fl...  3.76 us
    ppermute x1, starting transfers between devices, swap_far(): return lax.ppermute(cells, 'tile', pairs)  2.09 us
    dynamic_slice x1, local copies, waits for them, and re-layouts, local(): lax.dynamic_slice_in_dim(seeds, jnp.where(even, 0, tail), RIM, axis=2)  0.99 us
    ppermute x1, waiting for transfers between devices, swap_near(): return lax.ppermute(cells, 'tile', [(i, i ^ 1) for i in range(count)])  0.41 us
  transfers between devices with their start and end apart: 4, of which 1 were waited for; matrix products, arithmetic and copies ran while one was open for 6% of the time, Pallas kernels for 0%

profile of v6, /device:TPU:0, one launch (start us, length us, event | category | flops | bytes accessed | tf_op | source)
XLA Modules:
  0.0 19.7 jit_solution(12992531908073956256)
XLA Ops:
  0.0 2.9 %collective-permute-start.3 = (f32[2,5,8,128]{3,2,1,0:T(8,128)}, f32[2,5,8,128]{3,2,1,0:T(8,128)S(1)}, u32[]{:S(2)}, u32[]{:S(2)}) collective-permute-start(f32[2,5,8,128]{3,2,1,0:T(8,128)} %param.3), channel_id=1, source_target_pairs={{0,4},{4,8},{8,12},{12,16},{16,20},{20,24},{24,28},{28,0},{1,5},{5... | collective-permute-start | bytes 122888 | tf_op jit(solution)/shard_map/ppermute | solution.py:36
  2.9 3.0 %collective-permute-start.2 = (f32[2,5,8,128]{3,2,1,0:T(8,128)}, f32[2,5,8,128]{3,2,1,0:T(8,128)S(1)}, u32[]{:S(2)}, u32[]{:S(2)}) collective-permute-start(f32[2,5,8,128]{3,2,1,0:T(8,128)} %param.3), channel_id=1, source_target_pairs={{0,28},{4,0},{8,4},{12,8},{16,12},{20,16},{24,20},{28,24},{1,29},{... | collective-permute-start | bytes 122888 | tf_op jit(solution)/shard_map/ppermute | solution.py:36
  6.0 0.0 copy-start.1
  6.0 1.0 %constant_dynamic-slice_fusion = (f32[3,5,16,128]{3,2,1,0:T(8,128)S(1)}, f32[3,5,16,128]{3,2,1,0:T(8,128)S(1)}) fusion(f32[3,5,32,128]{3,2,1,0:T(8,128)} %seeds_ref.1, s32[]{:T(128)S(6)} %select_n.29, s32[]{:T(128)S(6)} %select_n.28), kind=kLoop, calls=%fused_computation.9 | loop fusion | bytes 491528 | tf_op jit(solution)/shard_map/dynamic_slice | solution.py:296
  7.0 2.1 %collective-permute-start.1 = (f32[3,5,16,128]{3,2,1,0:T(8,128)S(1)}, f32[3,5,16,128]{3,2,1,0:T(8,128)S(1)}, u32[]{:S(2)}, u32[]{:S(2)}) collective-permute-start(f32[3,5,16,128]{3,2,1,0:T(8,128)S(1)} %get-tuple-element.9), channel_id=1, source_target_pairs={{0,28},{4,8},{8,4},{12,16},{16,12},{20,24},{24,20},{28,0},{1,29},{... | collective-permute-start | bytes 368648 | tf_op jit(solution)/shard_map/ppermute | solution.py:42
  9.1 0.0 collective-permute-start
  9.1 0.0 copy-done.1
  9.1 0.0 collective-permute-done.2
  9.1 0.0 collective-permute-done.3
  9.2 0.1 fusion.1
  9.2 0.0 copy-start
  9.2 6.3 %all_gather.10.blocks_ref = f32[4,20,8,128]{3,2,1,0:T(8,128)S(1)} all-gather(f32[1,20,8,128]{3,2,1,0:T(8,128)S(1)} %fusion), channel_id=1, replica_groups=mesh['tile'=8,'func'=4] {'func'}, dimensions={0}, use_global_device_ids=true | all-gather | bytes 409600 | tf_op jit(solution)/shard_map/all_gather | solution.py:309
  15.5 0.0 collective-permute-done.1.far_ref
  15.5 0.4 %collective-permute-done.near_ref = f32[3,5,16,128]{3,2,1,0:T(8,128)S(1)} collective-permute-done((f32[3,5,16,128]{3,2,1,0:T(8,128)S(1)}, f32[3,5,16,128]{3,2,1,0:T(8,128)S(1)}, u32[]{:S(2)}, u32[]{:S(2)}) %collective-permute-start) | collective-permute-done | bytes 122912 | tf_op jit(solution)/shard_map/ppermute | solution.py:31
  15.9 0.0 copy-done
  15.9 3.8 %two_steps.1 = f32[3,5,32,128]{3,2,1,0:T(8,128)} custom-call(f32[3,5,32,128]{3,2,1,0:T(8,128)S(1)} %copy-done, f32[3,5,16,128]{3,2,1,0:T(8,128)S(1)} %collective-permute-done.near_ref, f32[3,5,16,128]{3,2,1,0:T(8,128)S(1)} %collective-permute-done.1.far_ref, f32[4,20,8,128]{3,2,1,0:T(8,128)S(1)} %all_gather.10.blocks_ref), custom_call_target="tpu_custom_call" | custom-call | tf_op jit(solution)/shard_map/two_steps/pallas_call | solution.py:323
  (5 shorter events, 0.0 us)
Async XLA Ops:
  0.0 9.1 %collective-permute-start.3 = (f32[2,5,8,128]{3,2,1,0:T(8,128)}, f32[2,5,8,128]{3,2,1,0:T(8,128)S(1)}, u32[]{:S(2)}, u32[]{:S(2)}) collective-permute-start(f32[2,5,8,128]{3,2,1,0:T(8,128)} %param.3), channel_id=1, source_target_pairs={{0,4},{4,8},{8,12},{12,16},{16,20},{20,24},{24,28},{28,0},{1,5},{5... | collective-permute-start | bytes 122888 | tf_op jit(solution)/shard_map/ppermute | solution.py:36
  2.9 6.2 %collective-permute-start.2 = (f32[2,5,8,128]{3,2,1,0:T(8,128)}, f32[2,5,8,128]{3,2,1,0:T(8,128)S(1)}, u32[]{:S(2)}, u32[]{:S(2)}) collective-permute-start(f32[2,5,8,128]{3,2,1,0:T(8,128)} %param.3), channel_id=1, source_target_pairs={{0,28},{4,0},{8,4},{12,8},{16,12},{20,16},{24,20},{28,24},{1,29},{... | collective-permute-start | bytes 122888 | tf_op jit(solution)/shard_map/ppermute | solution.py:36
  6.0 3.1 %copy-start.1 = (f32[2,5,8,128]{3,2,1,0:T(8,128)S(1)}, f32[2,5,8,128]{3,2,1,0:T(8,128)}, u32[]{:S(2)}) copy-start(f32[2,5,8,128]{3,2,1,0:T(8,128)} %param.3) | copy-start | bytes 122884
  7.0 8.5 %collective-permute-start.1 = (f32[3,5,16,128]{3,2,1,0:T(8,128)S(1)}, f32[3,5,16,128]{3,2,1,0:T(8,128)S(1)}, u32[]{:S(2)}, u32[]{:S(2)}) collective-permute-start(f32[3,5,16,128]{3,2,1,0:T(8,128)S(1)} %get-tuple-element.9), channel_id=1, source_target_pairs={{0,28},{4,8},{8,4},{12,16},{16,12},{20,24},{24,20},{28,0},{1,29},{... | collective-permute-start | bytes 368648 | tf_op jit(solution)/shard_map/ppermute | solution.py:42
  9.1 6.9 %collective-permute-start = (f32[3,5,16,128]{3,2,1,0:T(8,128)S(1)}, f32[3,5,16,128]{3,2,1,0:T(8,128)S(1)}, u32[]{:S(2)}, u32[]{:S(2)}) collective-permute-start(f32[3,5,16,128]{3,2,1,0:T(8,128)S(1)} %get-tuple-element.10), channel_id=1, source_target_pairs={{0,4},{4,0},{8,12},{12,8},{16,20},{20,16},{24,28},{28,24},{1,5},{5... | collective-permute-start | bytes 368648 | tf_op jit(solution)/shard_map/ppermute | solution.py:31
  9.2 6.7 %copy-start = (f32[3,5,32,128]{3,2,1,0:T(8,128)S(1)}, f32[3,5,32,128]{3,2,1,0:T(8,128)}, u32[]{:S(2)}) copy-start(f32[3,5,32,128]{3,2,1,0:T(8,128)} %seeds_ref.1) | copy-start | bytes 737284

commit v7 on v6

--- a/solution.py
+++ b/solution.py
@@ -2,6 +2,7 @@
 
 import jax
 import jax.numpy as jnp
+import numpy as np
 from jax import lax
 from jax.experimental import pallas as pl
 from jax.experimental.pallas import tpu as pltpu
@@ -42,25 +43,38 @@
     return lax.ppermute(cells, "tile", pairs)
 
 
+def banded(ahead):
+    weights = np.zeros(ahead.shape, np.float32)
+    for places, weight in ((1, 8.0), (-1, -8.0), (2, -1.0), (-2, 1.0)):
+        weights[ahead == places] = weight
+    return weights
+
+
 def second_weights():
-    shape = (LANES, LANES)
-    ahead = lax.broadcasted_iota(jnp.int32, shape, 0) - lax.broadcasted_iota(jnp.int32, shape, 1)
-    ahead = jnp.bitwise_and(ahead, LANES - 1)
-    weights = jnp.zeros(shape, jnp.float32)
-    for places, weight in ((NZ, 8.0), (-NZ, -8.0), (2 * NZ, -1.0), (-2 * NZ, 1.0)):
-        weights = jnp.where(ahead == places % LANES, weight, weights)
-    return jnp.concatenate([weights, weights], axis=0).astype(jnp.bfloat16)
+    place = np.arange(LANES)
+    ahead = (place[:, None] - place[None, :] + LANES // 2) % LANES - LANES // 2
+    weights = banded(np.where(ahead % NZ == 0, ahead // NZ, LANES))
+    return np.concatenate([weights, weights])
 
 
 def first_weights(count, total, skip):
-    shape = (count, 2 * total)
-    column = lax.broadcasted_iota(jnp.int32, shape, 1)
-    column = jnp.where(column < total, column, column - total)
-    ahead = column - lax.broadcasted_iota(jnp.int32, shape, 0) - skip
-    weights = jnp.zeros(shape, jnp.float32)
-    for places, weight in ((1, 8.0), (-1, -8.0), (2, -1.0), (-2, 1.0)):
-        weights = jnp.where(ahead == places, weight, weights)
-    return weights.astype(jnp.bfloat16)
+    weights = banded(np.arange(total)[None, :] - np.arange(count)[:, None] - skip)
+    return np.concatenate([weights, weights], axis=1)
+
+
+def all_weights(tall, span):
+    sizes = {(tall - 2 * start, tall - 2 * start) for start in range(0, STEPS * SUB, SUB)}
+    sizes |= {(tall - 2 * start - 2 * SUB, tall - 2 * start) for start in range(0, STEPS * SUB, SUB)}
+    for edges in STATE_EDGES:
+        sizes |= {(span - 2 * edges[n + 1], span - 2 * edges[n]) for n in range(3)}
+    width = -(-2 * span // LANES) * LANES
+    pieces, places, row = [], {}, 0
+    second = second_weights()
+    for piece, size in [(second, None)] + [(first_weights(*s, (s[1] - s[0]) // 2), s) for s in sorted(sizes)]:
+        places[size] = row
+        pieces.append(np.pad(piece, ((0, 0), (0, width - piece.shape[1]))))
+        row += piece.shape[0]
+    return np.concatenate(pieces), places
 
 
 def parts(cells):
@@ -204,7 +218,7 @@
 
 
 def kernel(
-    seeds_ref, near_ref, far_ref, blocks_ref, out_ref,
+    seeds_ref, near_ref, far_ref, blocks_ref, weights_ref, out_ref,
     adj_ref, hold_ref, first_ref, second_ref,
     base_ref, coef_ref, now_ref, flux_ref, slope_ref,
 ):
@@ -244,12 +258,12 @@
     lay_base(3, 1, strip, middle, min(LONG_RIM, strip - SHORT_RIM))
     lay_base(3, 0, -strip, strip - SHORT_RIM, strip)
 
-    weights = second_weights()
-    sizes = {(tall - 2 * start, tall - 2 * start) for start in range(0, STEPS * SUB, SUB)}
-    sizes |= {(tall - 2 * start - 2 * SUB, tall - 2 * start) for start in range(0, STEPS * SUB, SUB)}
-    for edges in STATE_EDGES:
-        sizes |= {(span - 2 * edges[n + 1], span - 2 * edges[n]) for n in range(3)}
-    lefts = {size: first_weights(*size, (size[1] - size[0]) // 2) for size in sorted(sizes)}
+    _, places = all_weights(tall, span)
+    weights = weights_ref[places[None] : places[None] + 2 * LANES, :LANES]
+    lefts = {
+        size: weights_ref[row : row + size[0], : 2 * size[1]] for size, row in places.items() if size is not None
+    }
+
     def states(moment):
         for stage in range(4):
             yield from state_stage(
@@ -323,12 +337,12 @@
     return pl.pallas_call(
         kernel,
         out_shape=jax.ShapeDtypeStruct(seeds.shape, jnp.float32),
-        in_specs=[vmem] * 4,
+        in_specs=[vmem] * 5,
         out_specs=vmem,
         scratch_shapes=[pltpu.VMEM(shape, jnp.float32) for shape in shapes],
         compiler_params=pltpu.CompilerParams(vmem_limit_bytes=32 * 1024 * 1024),
         name="two_steps",
-    )(seeds, near, far, blocks)
+    )(seeds, near, far, blocks, jnp.asarray(all_weights(tall, span)[0], jnp.bfloat16))
 
 
 def solution(mesh):

time: 19.8 us -> 19.8 us (level)
  no operation moved by 1% of the time
where the time goes in v7:
time: 19.8 us; the launch traced here: 19.6 us
  starting transfers between devices  8.07 us (41%)
  blocking collectives  6.26 us (32%)
  Pallas kernels  3.7 us (19%)
  local copies, waits for them, and re-layouts  1.01 us (5%)
  waiting for transfers between devices  0.41 us (2%)
    all_gather x1, blocking collectives, local(): blocks = lax.all_gather(packed, 'func', axis=0, tiled=False)  6.26 us
    ppermute x2, starting transfers between devices, shift(): lax.ppermute(cells, 'tile', [(i, (i + places) % count) for i in range(cou...  5.98 us
    pallas_call x1, Pallas kernels, local(): pl.pallas_call(kernel, out_shape=jax.ShapeDtypeStruct(seeds.shape, jnp.fl...  3.7 us
    ppermute x1, starting transfers between devices, swap_far(): return lax.ppermute(cells, 'tile', pairs)  2.09 us
    dynamic_slice x1, local copies, waits for them, and re-layouts, local(): lax.dynamic_slice_in_dim(seeds, jnp.where(even, 0, tail), RIM, axis=2)  0.99 us
    ppermute x1, waiting for transfers between devices, swap_near(): return lax.ppermute(cells, 'tile', [(i, i ^ 1) for i in range(count)])  0.4 us
  transfers between devices with their start and end apart: 4, of which 1 were waited for; matrix products, arithmetic and copies ran while one was open for 6% of the time, Pallas kernels for 0%

profile of v7, /device:TPU:0, one launch (start us, length us, event | category | flops | bytes accessed | tf_op | source)
XLA Modules:
  0.0 19.6 jit_solution(12664131856391099910)
XLA Ops:
  0.0 2.9 %collective-permute-start.3 = (f32[2,5,8,128]{3,2,1,0:T(8,128)}, f32[2,5,8,128]{3,2,1,0:T(8,128)S(1)}, u32[]{:S(2)}, u32[]{:S(2)}) collective-permute-start(f32[2,5,8,128]{3,2,1,0:T(8,128)} %param.4), channel_id=1, source_target_pairs={{0,4},{4,8},{8,12},{12,16},{16,20},{20,24},{24,28},{28,0},{1,5},{5... | collective-permute-start | bytes 122888 | tf_op jit(solution)/shard_map/ppermute | solution.py:37
  2.9 3.0 %collective-permute-start.2 = (f32[2,5,8,128]{3,2,1,0:T(8,128)}, f32[2,5,8,128]{3,2,1,0:T(8,128)S(1)}, u32[]{:S(2)}, u32[]{:S(2)}) collective-permute-start(f32[2,5,8,128]{3,2,1,0:T(8,128)} %param.4), channel_id=1, source_target_pairs={{0,28},{4,0},{8,4},{12,8},{16,12},{20,16},{24,20},{28,24},{1,29},{... | collective-permute-start | bytes 122888 | tf_op jit(solution)/shard_map/ppermute | solution.py:37
  6.0 0.0 copy-start.2
  6.0 1.0 %constant_dynamic-slice_fusion = (f32[3,5,16,128]{3,2,1,0:T(8,128)S(1)}, f32[3,5,16,128]{3,2,1,0:T(8,128)S(1)}) fusion(f32[3,5,32,128]{3,2,1,0:T(8,128)} %seeds_ref.1, s32[]{:T(128)S(6)} %select_n.29, s32[]{:T(128)S(6)} %select_n.28), kind=kLoop, calls=%fused_computation.9 | loop fusion | bytes 491528 | tf_op jit(solution)/shard_map/dynamic_slice | solution.py:310
  7.0 2.1 %collective-permute-start.1 = (f32[3,5,16,128]{3,2,1,0:T(8,128)S(1)}, f32[3,5,16,128]{3,2,1,0:T(8,128)S(1)}, u32[]{:S(2)}, u32[]{:S(2)}) collective-permute-start(f32[3,5,16,128]{3,2,1,0:T(8,128)S(1)} %get-tuple-element.9), channel_id=1, source_target_pairs={{0,28},{4,8},{8,4},{12,16},{16,12},{20,24},{24,20},{28,0},{1,29},{... | collective-permute-start | bytes 368648 | tf_op jit(solution)/shard_map/ppermute | solution.py:43
  9.1 0.0 collective-permute-start
  9.1 0.0 copy-done.2
  9.1 0.0 collective-permute-done.2
  9.1 0.0 collective-permute-done.3
  9.1 0.0 copy-start.1
  9.2 0.1 fusion.1
  9.2 0.0 copy-start
  9.3 6.3 %all_gather.10.blocks_ref = f32[4,20,8,128]{3,2,1,0:T(8,128)S(1)} all-gather(f32[1,20,8,128]{3,2,1,0:T(8,128)S(1)} %fusion), channel_id=1, replica_groups=mesh['tile'=8,'func'=4] {'func'}, dimensions={0}, use_global_device_ids=true | all-gather | bytes 409600 | tf_op jit(solution)/shard_map/all_gather | solution.py:323
  15.5 0.0 collective-permute-done.1.far_ref
  15.5 0.4 %collective-permute-done.near_ref = f32[3,5,16,128]{3,2,1,0:T(8,128)S(1)} collective-permute-done((f32[3,5,16,128]{3,2,1,0:T(8,128)S(1)}, f32[3,5,16,128]{3,2,1,0:T(8,128)S(1)}, u32[]{:S(2)}, u32[]{:S(2)}) %collective-permute-start) | collective-permute-done | bytes 122912 | tf_op jit(solution)/shard_map/ppermute | solution.py:32
  15.9 0.0 copy-done.1
  15.9 0.0 copy-done
  15.9 3.7 %two_steps.1 = f32[3,5,32,128]{3,2,1,0:T(8,128)} custom-call(f32[3,5,32,128]{3,2,1,0:T(8,128)S(1)} %copy-done, f32[3,5,16,128]{3,2,1,0:T(8,128)S(1)} %collective-permute-done.near_ref, f32[3,5,16,128]{3,2,1,0:T(8,128)S(1)} %collective-permute-done.1.far_ref, f32[4,20,8,128]{3,2,1,0:T(8,128)S(1)} %all_gather.10.blocks_ref, bf16[592,256]{1,0:T(8,128)(2,1)S(1)} %copy-done.1), custom_call_target="tpu_custom_call" | custom-call | tf_op jit(solution)/shard_map/two_steps/pallas_call | solution.py:337
  (5 shorter events, 0.0 us)
Async XLA Ops:
  0.0 9.1 %collective-permute-start.3 = (f32[2,5,8,128]{3,2,1,0:T(8,128)}, f32[2,5,8,128]{3,2,1,0:T(8,128)S(1)}, u32[]{:S(2)}, u32[]{:S(2)}) collective-permute-start(f32[2,5,8,128]{3,2,1,0:T(8,128)} %param.4), channel_id=1, source_target_pairs={{0,4},{4,8},{8,12},{12,16},{16,20},{20,24},{24,28},{28,0},{1,5},{5... | collective-permute-start | bytes 122888 | tf_op jit(solution)/shard_map/ppermute | solution.py:37
  2.9 6.2 %collective-permute-start.2 = (f32[2,5,8,128]{3,2,1,0:T(8,128)}, f32[2,5,8,128]{3,2,1,0:T(8,128)S(1)}, u32[]{:S(2)}, u32[]{:S(2)}) collective-permute-start(f32[2,5,8,128]{3,2,1,0:T(8,128)} %param.4), channel_id=1, source_target_pairs={{0,28},{4,0},{8,4},{12,8},{16,12},{20,16},{24,20},{28,24},{1,29},{... | collective-permute-start | bytes 122888 | tf_op jit(solution)/shard_map/ppermute | solution.py:37
  6.0 3.1 %copy-start.2 = (f32[2,5,8,128]{3,2,1,0:T(8,128)S(1)}, f32[2,5,8,128]{3,2,1,0:T(8,128)}, u32[]{:S(2)}) copy-start(f32[2,5,8,128]{3,2,1,0:T(8,128)} %param.4) | copy-start | bytes 122884
  7.0 8.5 %collective-permute-start.1 = (f32[3,5,16,128]{3,2,1,0:T(8,128)S(1)}, f32[3,5,16,128]{3,2,1,0:T(8,128)S(1)}, u32[]{:S(2)}, u32[]{:S(2)}) collective-permute-start(f32[3,5,16,128]{3,2,1,0:T(8,128)S(1)} %get-tuple-element.9), channel_id=1, source_target_pairs={{0,28},{4,8},{8,4},{12,16},{16,12},{20,24},{24,20},{28,0},{1,29},{... | collective-permute-start | bytes 368648 | tf_op jit(solution)/shard_map/ppermute | solution.py:43
  9.1 6.9 %collective-permute-start = (f32[3,5,16,128]{3,2,1,0:T(8,128)S(1)}, f32[3,5,16,128]{3,2,1,0:T(8,128)S(1)}, u32[]{:S(2)}, u32[]{:S(2)}) collective-permute-start(f32[3,5,16,128]{3,2,1,0:T(8,128)S(1)} %get-tuple-element.10), channel_id=1, source_target_pairs={{0,4},{4,0},{8,12},{12,8},{16,20},{20,16},{24,28},{28,24},{1,5},{5... | collective-permute-start | bytes 368648 | tf_op jit(solution)/shard_map/ppermute | solution.py:32
  9.1 6.8 %copy-start.1 = (bf16[592,256]{1,0:T(8,128)(2,1)S(1)}, bf16[592,256]{1,0:T(8,128)(2,1)}, u32[]{:S(2)}) copy-start(bf16[592,256]{1,0:T(8,128)(2,1)} %constant.33.clone.weights_ref) | copy-start | bytes 909316
  9.2 6.7 %copy-start = (f32[3,5,32,128]{3,2,1,0:T(8,128)S(1)}, f32[3,5,32,128]{3,2,1,0:T(8,128)}, u32[]{:S(2)}) copy-start(f32[3,5,32,128]{3,2,1,0:T(8,128)} %seeds_ref.1) | copy-start | bytes 737284

commit v8 on v7

--- a/solution.py
+++ b/solution.py
@@ -227,12 +227,6 @@
     tall, span = strip + 2 * RIM, strip + 2 * BASE_RIM
     even = lax.rem(lax.axis_index("tile"), 2) == 0
 
-    def lay(left_ref, right_ref):
-        for one in range(funcs):
-            for k in range(FIELDS):
-                adj_ref[one, k, :RIM] = left_ref[one, k]
-                adj_ref[one, k, RIM + strip :] = right_ref[one, k]
-
     def lay_base(part, moment, shift, low, high):
         for owner in range(spread):
             start, stop = max(low, owner * block), min(high, (owner + 1) * block)
@@ -273,8 +267,11 @@
     def differences(moment, stage, one):
         return pull_differences(moment, stage, one, adj_ref, hold_ref, first_ref, second_ref, lefts, weights)
 
-    pl.when(even)(lambda: lay(far_ref, near_ref))
-    pl.when(jnp.logical_not(even))(lambda: lay(near_ref, far_ref))
+    for one in range(funcs):
+        for k in range(FIELDS):
+            near, far = near_ref[one, k], far_ref[one, k]
+            adj_ref[one, k, :RIM] = jnp.where(even, far, near)
+            adj_ref[one, k, RIM + strip :] = jnp.where(even, near, far)
     for one in range(funcs):
         for k in range(FIELDS):
             adj_ref[one, k, RIM : RIM + strip] = seeds_ref[one, k]

time: 19.8 us -> 19.7 us (level)
  no operation moved by 1% of the time
where the time goes in v8:
time: 19.7 us; the launch traced here: 19.5 us
  starting transfers between devices  8.07 us (41%)
  blocking collectives  6.26 us (32%)
  Pallas kernels  3.61 us (18%)
  local copies, waits for them, and re-layouts  1.01 us (5%)
  waiting for transfers between devices  0.41 us (2%)
    all_gather x1, blocking collectives, local(): blocks = lax.all_gather(packed, 'func', axis=0, tiled=False)  6.26 us
    ppermute x2, starting transfers between devices, shift(): lax.ppermute(cells, 'tile', [(i, (i + places) % count) for i in range(cou...  5.98 us
    pallas_call x1, Pallas kernels, local(): pl.pallas_call(kernel, out_shape=jax.ShapeDtypeStruct(seeds.shape, jnp.fl...  3.61 us
    ppermute x1, starting transfers between devices, swap_far(): return lax.ppermute(cells, 'tile', pairs)  2.09 us
    dynamic_slice x1, local copies, waits for them, and re-layouts, local(): lax.dynamic_slice_in_dim(seeds, jnp.where(even, 0, tail), RIM, axis=2)  0.99 us
    ppermute x1, waiting for transfers between devices, swap_near(): return lax.ppermute(cells, 'tile', [(i, i ^ 1) for i in range(count)])  0.4 us
  transfers between devices with their start and end apart: 4, of which 1 were waited for; matrix products, arithmetic and copies ran while one was open for 6% of the time, Pallas kernels for 0%

profile of v8, /device:TPU:0, one launch (start us, length us, event | category | flops | bytes accessed | tf_op | source)
XLA Modules:
  0.0 19.5 jit_solution(6400390886526181650)
XLA Ops:
  0.0 2.9 %collective-permute-start.3 = (f32[2,5,8,128]{3,2,1,0:T(8,128)}, f32[2,5,8,128]{3,2,1,0:T(8,128)S(1)}, u32[]{:S(2)}, u32[]{:S(2)}) collective-permute-start(f32[2,5,8,128]{3,2,1,0:T(8,128)} %param.4), channel_id=1, source_target_pairs={{0,4},{4,8},{8,12},{12,16},{16,20},{20,24},{24,28},{28,0},{1,5},{5... | collective-permute-start | bytes 122888 | tf_op jit(solution)/shard_map/ppermute | solution.py:37
  2.9 3.0 %collective-permute-start.2 = (f32[2,5,8,128]{3,2,1,0:T(8,128)}, f32[2,5,8,128]{3,2,1,0:T(8,128)S(1)}, u32[]{:S(2)}, u32[]{:S(2)}) collective-permute-start(f32[2,5,8,128]{3,2,1,0:T(8,128)} %param.4), channel_id=1, source_target_pairs={{0,28},{4,0},{8,4},{12,8},{16,12},{20,16},{24,20},{28,24},{1,29},{... | collective-permute-start | bytes 122888 | tf_op jit(solution)/shard_map/ppermute | solution.py:37
  6.0 0.0 copy-start.2
  6.0 1.0 %constant_dynamic-slice_fusion = (f32[3,5,16,128]{3,2,1,0:T(8,128)S(1)}, f32[3,5,16,128]{3,2,1,0:T(8,128)S(1)}) fusion(f32[3,5,32,128]{3,2,1,0:T(8,128)} %seeds_ref.1, s32[]{:T(128)S(6)} %select_n.29, s32[]{:T(128)S(6)} %select_n.28), kind=kLoop, calls=%fused_computation.9 | loop fusion | bytes 491528 | tf_op jit(solution)/shard_map/dynamic_slice | solution.py:307
  7.0 2.1 %collective-permute-start.1 = (f32[3,5,16,128]{3,2,1,0:T(8,128)S(1)}, f32[3,5,16,128]{3,2,1,0:T(8,128)S(1)}, u32[]{:S(2)}, u32[]{:S(2)}) collective-permute-start(f32[3,5,16,128]{3,2,1,0:T(8,128)S(1)} %get-tuple-element.9), channel_id=1, source_target_pairs={{0,28},{4,8},{8,4},{12,16},{16,12},{20,24},{24,20},{28,0},{1,29},{... | collective-permute-start | bytes 368648 | tf_op jit(solution)/shard_map/ppermute | solution.py:43
  9.1 0.0 collective-permute-start
  9.1 0.0 copy-done.2
  9.1 0.0 collective-permute-done.2
  9.1 0.0 collective-permute-done.3
  9.1 0.0 copy-start.1
  9.2 0.1 fusion.1
  9.2 0.0 copy-start
  9.3 6.3 %all_gather.10.blocks_ref = f32[4,20,8,128]{3,2,1,0:T(8,128)S(1)} all-gather(f32[1,20,8,128]{3,2,1,0:T(8,128)S(1)} %fusion), channel_id=1, replica_groups=mesh['tile'=8,'func'=4] {'func'}, dimensions={0}, use_global_device_ids=true | all-gather | bytes 409600 | tf_op jit(solution)/shard_map/all_gather | solution.py:320
  15.5 0.0 collective-permute-done.1.far_ref
  15.5 0.4 %collective-permute-done.near_ref = f32[3,5,16,128]{3,2,1,0:T(8,128)S(1)} collective-permute-done((f32[3,5,16,128]{3,2,1,0:T(8,128)S(1)}, f32[3,5,16,128]{3,2,1,0:T(8,128)S(1)}, u32[]{:S(2)}, u32[]{:S(2)}) %collective-permute-start) | collective-permute-done | bytes 122912 | tf_op jit(solution)/shard_map/ppermute | solution.py:32
  15.9 0.0 copy-done.1
  15.9 0.0 copy-done
  15.9 3.6 %two_steps.1 = f32[3,5,32,128]{3,2,1,0:T(8,128)} custom-call(f32[3,5,32,128]{3,2,1,0:T(8,128)S(1)} %copy-done, f32[3,5,16,128]{3,2,1,0:T(8,128)S(1)} %collective-permute-done.near_ref, f32[3,5,16,128]{3,2,1,0:T(8,128)S(1)} %collective-permute-done.1.far_ref, f32[4,20,8,128]{3,2,1,0:T(8,128)S(1)} %all_gather.10.blocks_ref, bf16[592,256]{1,0:T(8,128)(2,1)S(1)} %copy-done.1), custom_call_target="tpu_custom_call" | custom-call | tf_op jit(solution)/shard_map/two_steps/pallas_call | solution.py:334
  (5 shorter events, 0.0 us)
Async XLA Ops:
  0.0 9.1 %collective-permute-start.3 = (f32[2,5,8,128]{3,2,1,0:T(8,128)}, f32[2,5,8,128]{3,2,1,0:T(8,128)S(1)}, u32[]{:S(2)}, u32[]{:S(2)}) collective-permute-start(f32[2,5,8,128]{3,2,1,0:T(8,128)} %param.4), channel_id=1, source_target_pairs={{0,4},{4,8},{8,12},{12,16},{16,20},{20,24},{24,28},{28,0},{1,5},{5... | collective-permute-start | bytes 122888 | tf_op jit(solution)/shard_map/ppermute | solution.py:37
  2.9 6.2 %collective-permute-start.2 = (f32[2,5,8,128]{3,2,1,0:T(8,128)}, f32[2,5,8,128]{3,2,1,0:T(8,128)S(1)}, u32[]{:S(2)}, u32[]{:S(2)}) collective-permute-start(f32[2,5,8,128]{3,2,1,0:T(8,128)} %param.4), channel_id=1, source_target_pairs={{0,28},{4,0},{8,4},{12,8},{16,12},{20,16},{24,20},{28,24},{1,29},{... | collective-permute-start | bytes 122888 | tf_op jit(solution)/shard_map/ppermute | solution.py:37
  6.0 3.1 %copy-start.2 = (f32[2,5,8,128]{3,2,1,0:T(8,128)S(1)}, f32[2,5,8,128]{3,2,1,0:T(8,128)}, u32[]{:S(2)}) copy-start(f32[2,5,8,128]{3,2,1,0:T(8,128)} %param.4) | copy-start | bytes 122884
  7.0 8.5 %collective-permute-start.1 = (f32[3,5,16,128]{3,2,1,0:T(8,128)S(1)}, f32[3,5,16,128]{3,2,1,0:T(8,128)S(1)}, u32[]{:S(2)}, u32[]{:S(2)}) collective-permute-start(f32[3,5,16,128]{3,2,1,0:T(8,128)S(1)} %get-tuple-element.9), channel_id=1, source_target_pairs={{0,28},{4,8},{8,4},{12,16},{16,12},{20,24},{24,20},{28,0},{1,29},{... | collective-permute-start | bytes 368648 | tf_op jit(solution)/shard_map/ppermute | solution.py:43
  9.1 6.9 %collective-permute-start = (f32[3,5,16,128]{3,2,1,0:T(8,128)S(1)}, f32[3,5,16,128]{3,2,1,0:T(8,128)S(1)}, u32[]{:S(2)}, u32[]{:S(2)}) collective-permute-start(f32[3,5,16,128]{3,2,1,0:T(8,128)S(1)} %get-tuple-element.10), channel_id=1, source_target_pairs={{0,4},{4,0},{8,12},{12,8},{16,20},{20,16},{24,28},{28,24},{1,5},{5... | collective-permute-start | bytes 368648 | tf_op jit(solution)/shard_map/ppermute | solution.py:32
  9.1 6.8 %copy-start.1 = (bf16[592,256]{1,0:T(8,128)(2,1)S(1)}, bf16[592,256]{1,0:T(8,128)(2,1)}, u32[]{:S(2)}) copy-start(bf16[592,256]{1,0:T(8,128)(2,1)} %constant.33.clone.weights_ref) | copy-start | bytes 909316
  9.2 6.7 %copy-start = (f32[3,5,32,128]{3,2,1,0:T(8,128)S(1)}, f32[3,5,32,128]{3,2,1,0:T(8,128)}, u32[]{:S(2)}) copy-start(f32[3,5,32,128]{3,2,1,0:T(8,128)} %seeds_ref.1) | copy-start | bytes 737284

commit v9 on v8

--- a/solution.py
+++ b/solution.py
@@ -22,7 +22,7 @@
 LONG_RIM = 20
 SHORT_RIM = 12
 STATE_RIMS = (SHORT_RIM, LONG_RIM)
-START_EVERY, STORES = 2, 2
+START_EVERY, STORES = 2, 1
 STILL = (1.0, 0.0, 0.0, 0.0, 2.5)
 STATE_EDGES = ((8, 8, 16, 16), (0, 0, 8, 8))
 

time: 19.7 us -> 19.7 us (level)
  no operation moved by 1% of the time
where the time goes in v9:
time: 19.7 us; the launch traced here: 19.5 us
  starting transfers between devices  8.07 us (41%)
  blocking collectives  6.26 us (32%)
  Pallas kernels  3.61 us (18%)
  local copies, waits for them, and re-layouts  1.01 us (5%)
  waiting for transfers between devices  0.41 us (2%)
    all_gather x1, blocking collectives, local(): blocks = lax.all_gather(packed, 'func', axis=0, tiled=False)  6.26 us
    ppermute x2, starting transfers between devices, shift(): lax.ppermute(cells, 'tile', [(i, (i + places) % count) for i in range(cou...  5.98 us
    pallas_call x1, Pallas kernels, local(): pl.pallas_call(kernel, out_shape=jax.ShapeDtypeStruct(seeds.shape, jnp.fl...  3.61 us
    ppermute x1, starting transfers between devices, swap_far(): return lax.ppermute(cells, 'tile', pairs)  2.09 us
    dynamic_slice x1, local copies, waits for them, and re-layouts, local(): lax.dynamic_slice_in_dim(seeds, jnp.where(even, 0, tail), RIM, axis=2)  0.99 us
    ppermute x1, waiting for transfers between devices, swap_near(): return lax.ppermute(cells, 'tile', [(i, i ^ 1) for i in range(count)])  0.4 us
  transfers between devices with their start and end apart: 4, of which 1 were waited for; matrix products, arithmetic and copies ran while one was open for 6% of the time, Pallas kernels for 0%

profile of v9, /device:TPU:0, one launch (start us, length us, event | category | flops | bytes accessed | tf_op | source)
XLA Modules:
  0.0 19.5 jit_solution(6400390886526181650)
XLA Ops:
  0.0 2.9 %collective-permute-start.3 = (f32[2,5,8,128]{3,2,1,0:T(8,128)}, f32[2,5,8,128]{3,2,1,0:T(8,128)S(1)}, u32[]{:S(2)}, u32[]{:S(2)}) collective-permute-start(f32[2,5,8,128]{3,2,1,0:T(8,128)} %param.4), channel_id=1, source_target_pairs={{0,4},{4,8},{8,12},{12,16},{16,20},{20,24},{24,28},{28,0},{1,5},{5... | collective-permute-start | bytes 122888 | tf_op jit(solution)/shard_map/ppermute | solution.py:37
  2.9 3.0 %collective-permute-start.2 = (f32[2,5,8,128]{3,2,1,0:T(8,128)}, f32[2,5,8,128]{3,2,1,0:T(8,128)S(1)}, u32[]{:S(2)}, u32[]{:S(2)}) collective-permute-start(f32[2,5,8,128]{3,2,1,0:T(8,128)} %param.4), channel_id=1, source_target_pairs={{0,28},{4,0},{8,4},{12,8},{16,12},{20,16},{24,20},{28,24},{1,29},{... | collective-permute-start | bytes 122888 | tf_op jit(solution)/shard_map/ppermute | solution.py:37
  6.0 0.0 copy-start.2
  6.0 1.0 %constant_dynamic-slice_fusion = (f32[3,5,16,128]{3,2,1,0:T(8,128)S(1)}, f32[3,5,16,128]{3,2,1,0:T(8,128)S(1)}) fusion(f32[3,5,32,128]{3,2,1,0:T(8,128)} %seeds_ref.1, s32[]{:T(128)S(6)} %select_n.29, s32[]{:T(128)S(6)} %select_n.28), kind=kLoop, calls=%fused_computation.9 | loop fusion | bytes 491528 | tf_op jit(solution)/shard_map/dynamic_slice | solution.py:307
  7.0 2.1 %collective-permute-start.1 = (f32[3,5,16,128]{3,2,1,0:T(8,128)S(1)}, f32[3,5,16,128]{3,2,1,0:T(8,128)S(1)}, u32[]{:S(2)}, u32[]{:S(2)}) collective-permute-start(f32[3,5,16,128]{3,2,1,0:T(8,128)S(1)} %get-tuple-element.9), channel_id=1, source_target_pairs={{0,28},{4,8},{8,4},{12,16},{16,12},{20,24},{24,20},{28,0},{1,29},{... | collective-permute-start | bytes 368648 | tf_op jit(solution)/shard_map/ppermute | solution.py:43
  9.1 0.0 collective-permute-start
  9.1 0.0 copy-done.2
  9.1 0.0 collective-permute-done.2
  9.1 0.0 collective-permute-done.3
  9.1 0.0 copy-start.1
  9.2 0.1 fusion.1
  9.2 0.0 copy-start
  9.3 6.3 %all_gather.10.blocks_ref = f32[4,20,8,128]{3,2,1,0:T(8,128)S(1)} all-gather(f32[1,20,8,128]{3,2,1,0:T(8,128)S(1)} %fusion), channel_id=1, replica_groups=mesh['tile'=8,'func'=4] {'func'}, dimensions={0}, use_global_device_ids=true | all-gather | bytes 409600 | tf_op jit(solution)/shard_map/all_gather | solution.py:320
  15.5 0.0 collective-permute-done.1.far_ref
  15.5 0.4 %collective-permute-done.near_ref = f32[3,5,16,128]{3,2,1,0:T(8,128)S(1)} collective-permute-done((f32[3,5,16,128]{3,2,1,0:T(8,128)S(1)}, f32[3,5,16,128]{3,2,1,0:T(8,128)S(1)}, u32[]{:S(2)}, u32[]{:S(2)}) %collective-permute-start) | collective-permute-done | bytes 122912 | tf_op jit(solution)/shard_map/ppermute | solution.py:32
  15.9 0.0 copy-done.1
  15.9 0.0 copy-done
  15.9 3.6 %two_steps.1 = f32[3,5,32,128]{3,2,1,0:T(8,128)} custom-call(f32[3,5,32,128]{3,2,1,0:T(8,128)S(1)} %copy-done, f32[3,5,16,128]{3,2,1,0:T(8,128)S(1)} %collective-permute-done.near_ref, f32[3,5,16,128]{3,2,1,0:T(8,128)S(1)} %collective-permute-done.1.far_ref, f32[4,20,8,128]{3,2,1,0:T(8,128)S(1)} %all_gather.10.blocks_ref, bf16[592,256]{1,0:T(8,128)(2,1)S(1)} %copy-done.1), custom_call_target="tpu_custom_call" | custom-call | tf_op jit(solution)/shard_map/two_steps/pallas_call | solution.py:334
  (5 shorter events, 0.0 us)
Async XLA Ops:
  0.0 9.1 %collective-permute-start.3 = (f32[2,5,8,128]{3,2,1,0:T(8,128)}, f32[2,5,8,128]{3,2,1,0:T(8,128)S(1)}, u32[]{:S(2)}, u32[]{:S(2)}) collective-permute-start(f32[2,5,8,128]{3,2,1,0:T(8,128)} %param.4), channel_id=1, source_target_pairs={{0,4},{4,8},{8,12},{12,16},{16,20},{20,24},{24,28},{28,0},{1,5},{5... | collective-permute-start | bytes 122888 | tf_op jit(solution)/shard_map/ppermute | solution.py:37
  2.9 6.2 %collective-permute-start.2 = (f32[2,5,8,128]{3,2,1,0:T(8,128)}, f32[2,5,8,128]{3,2,1,0:T(8,128)S(1)}, u32[]{:S(2)}, u32[]{:S(2)}) collective-permute-start(f32[2,5,8,128]{3,2,1,0:T(8,128)} %param.4), channel_id=1, source_target_pairs={{0,28},{4,0},{8,4},{12,8},{16,12},{20,16},{24,20},{28,24},{1,29},{... | collective-permute-start | bytes 122888 | tf_op jit(solution)/shard_map/ppermute | solution.py:37
  6.0 3.1 %copy-start.2 = (f32[2,5,8,128]{3,2,1,0:T(8,128)S(1)}, f32[2,5,8,128]{3,2,1,0:T(8,128)}, u32[]{:S(2)}) copy-start(f32[2,5,8,128]{3,2,1,0:T(8,128)} %param.4) | copy-start | bytes 122884
  7.0 8.5 %collective-permute-start.1 = (f32[3,5,16,128]{3,2,1,0:T(8,128)S(1)}, f32[3,5,16,128]{3,2,1,0:T(8,128)S(1)}, u32[]{:S(2)}, u32[]{:S(2)}) collective-permute-start(f32[3,5,16,128]{3,2,1,0:T(8,128)S(1)} %get-tuple-element.9), channel_id=1, source_target_pairs={{0,28},{4,8},{8,4},{12,16},{16,12},{20,24},{24,20},{28,0},{1,29},{... | collective-permute-start | bytes 368648 | tf_op jit(solution)/shard_map/ppermute | solution.py:43
  9.1 6.9 %collective-permute-start = (f32[3,5,16,128]{3,2,1,0:T(8,128)S(1)}, f32[3,5,16,128]{3,2,1,0:T(8,128)S(1)}, u32[]{:S(2)}, u32[]{:S(2)}) collective-permute-start(f32[3,5,16,128]{3,2,1,0:T(8,128)S(1)} %get-tuple-element.10), channel_id=1, source_target_pairs={{0,4},{4,0},{8,12},{12,8},{16,20},{20,16},{24,28},{28,24},{1,5},{5... | collective-permute-start | bytes 368648 | tf_op jit(solution)/shard_map/ppermute | solution.py:32
  9.1 6.8 %copy-start.1 = (bf16[592,256]{1,0:T(8,128)(2,1)S(1)}, bf16[592,256]{1,0:T(8,128)(2,1)}, u32[]{:S(2)}) copy-start(bf16[592,256]{1,0:T(8,128)(2,1)} %constant.33.clone.weights_ref) | copy-start | bytes 909316
  9.2 6.7 %copy-start = (f32[3,5,32,128]{3,2,1,0:T(8,128)S(1)}, f32[3,5,32,128]{3,2,1,0:T(8,128)}, u32[]{:S(2)}) copy-start(f32[3,5,32,128]{3,2,1,0:T(8,128)} %seeds_ref.1) | copy-start | bytes 737284
